TPU v7x, 512 devices: a whole 4x4x16 slice. The times are simulated.
512 devices in a mesh: blk: 16 (over x, y_lo, core), dp: 32 (over y_hi, z).
Axes of the slice: x: 4, y: 4 (y_hi: 2, y_lo: 2; y = y_hi * 2 + y_lo), z: 16, core: 2. Of those that a mesh axis runs over, the one named last changes fastest.
Arguments:
- users: bfloat16 [32, 4096, 512], P('dp', 'blk'), may hold values from -32 to 32
- items: bfloat16 [32, 4096, 512], P('dp', 'blk'), may hold values from -24 to 24
- weights: float32 [32, 4096], P('dp', 'blk'), may hold values from 0.5 to 18
- positives: int32 [32, 4096], P('dp', 'blk'), may hold values from 0 to 4095, each once within a row
- log_scale: float32 [1], replicated, may hold values from 0 to 1.1
Outputs:
- grad_users: bfloat16 [32, 4096, 512], P('dp', 'blk')
- grad_items: bfloat16 [32, 4096, 512], P('dp', 'blk')
- scale_grad: float32 [1], replicated
Inputs may be any that keep to these rules, and one draw needn't show every extreme that they name: For each group g, positives[g] is a permutation of 0 to 4095.
All inputs are finite; a program needn't handle non-finite values.
Results may differ from a plain program's by a relative error of at most 0.0049.
Values may be sent and summed in bfloat16 or wider, within the bound.
A program may use at most 64 MiB of HBM per device.

v0:
```python
import math

import jax
import jax.numpy as jnp
from jax import lax
from jax.sharding import PartitionSpec as P


def shifted(block, axis, distance):
    devices = range(lax.axis_size(axis))
    route = [((i - distance) % len(devices), i) for i in devices]
    return lax.ppermute(block, axis, route)


def block_scores(user_rows, item_block, logit_scale):
    return logit_scale * jnp.einsum(
        "rd,cd->rc", user_rows, item_block, preferred_element_type=jnp.float32
    )


def target_hits(targets, first_item, lane_rows):
    columns = first_item + lax.iota(jnp.int32, lane_rows)
    return (targets[:, None] == columns[None, :]).astype(jnp.float32)


def first_move(travel):
    item_block = travel[0]
    item_block = shifted(item_block, "blk", 1)
    stats = shifted((travel[1], travel[2], travel[3]), "blk", 1)
    return (item_block, stats[0], stats[1], stats[2])


def second_move(travel):
    return (
        shifted(travel[0].astype(jnp.float32), "blk", -1).astype(jnp.bfloat16),
        shifted(travel[1], "blk", -1),
        shifted(travel[2], "blk", -1),
        shifted(travel[3], "blk", -1),
    )


def cycle_plan(user_rows, item_rows, weight_rows, targets, logit_scale, blk_index, blk_size):
    rows_here = user_rows.shape[0]
    width = user_rows.shape[1]
    lane_list = ((1, 0, rows_here),)

    def first_visit(carry, turn_index, moving):
        travels, row_max, row_total, stat_table = carry
        moved_list = []
        for lane_spec, travel in zip(lane_list, travels):
            direction, offset, lane_rows = lane_spec
            source = jnp.mod(blk_index - direction * turn_index, blk_size)
            first_item = source * rows_here + offset
            scores = block_scores(user_rows, travel[0], logit_scale)
            hits = target_hits(targets, first_item, lane_rows)
            new_max = jnp.maximum(row_max, jnp.max(scores, axis=1))
            row_total = row_total * jnp.exp(row_max - new_max) + jnp.sum(
                jnp.exp(scores - new_max[:, None]), axis=1
            )
            row_max = new_max
            col_max = jnp.max(scores, axis=0)
            col_total = jnp.sum(jnp.exp(scores - col_max[None, :]), axis=0)
            col_weight = jnp.sum(weight_rows[:, None] * hits, axis=0)
            joined_max = jnp.maximum(travel[1], col_max)
            summed = travel[2] * jnp.exp(travel[1] - joined_max) + col_total * jnp.exp(
                col_max - joined_max
            )
            travel = (travel[0], joined_max, summed, travel[3] + col_weight)
            if moving:
                travel = first_move(travel)
            moved_list.append(travel)
        return (tuple(moved_list), row_max, row_total, stat_table)

    travels = tuple(
        (
            (
                item_rows,
                jnp.full((lane_rows,), -jnp.inf, jnp.float32),
                jnp.zeros((lane_rows,), jnp.float32),
                jnp.zeros((lane_rows,), jnp.float32),
            )
            for direction, offset, lane_rows in lane_list
        )
    )
    stat_table = ()
    carry = (
        travels,
        jnp.full((rows_here,), -jnp.inf, jnp.float32),
        jnp.zeros((rows_here,), jnp.float32),
        stat_table,
    )
    carry = lax.fori_loop(
        0,
        blk_size - 1,
        lambda turn_index, state_now: first_visit(state_now, turn_index, True),
        carry,
    )
    travels, row_max, row_total, stat_table = first_visit(carry, blk_size - 1, False)
    row_lse = row_max + jnp.log(row_total)
    travels = tuple(
        (
            (
                travel[0],
                travel[1] + jnp.log(travel[2]),
                travel[3],
                jnp.zeros((travel[0].shape[0], width), jnp.float32),
            )
            for travel in travels
        )
    )

    def second_visit(carry, turn_index, moving):
        travels, user_grad, scale_part = carry
        moved_list = []
        for lane_spec, travel in zip(lane_list, travels):
            direction, offset, lane_rows = lane_spec
            source = jnp.mod(
                blk_index - direction * (blk_size - 1) + direction * turn_index, blk_size
            )
            first_item = source * rows_here + offset
            item_block = travel[0]
            col_lse = travel[1]
            col_weight = travel[2]
            item_grad = travel[3]
            scores = block_scores(user_rows, item_block, logit_scale)
            hits = target_hits(targets, first_item, lane_rows)
            score_grad = weight_rows[:, None] * (
                jnp.exp(scores - row_lse[:, None]) - hits
            ) + col_weight[None, :] * (jnp.exp(scores - col_lse[None, :]) - hits)
            rounded = score_grad.astype(jnp.bfloat16)
            user_grad = user_grad + jnp.dot(rounded, item_block, preferred_element_type=jnp.float32)
            item_grad = item_grad + jnp.einsum(
                "rc,rd->cd", rounded, user_rows, preferred_element_type=jnp.float32
            )
            scale_part = scale_part + jnp.sum(score_grad * scores)
            travel = (item_block, col_lse, col_weight, item_grad)
            if moving:
                travel = second_move(travel)
            moved_list.append(travel)
        return (tuple(moved_list), user_grad, scale_part)

    carry = (travels, jnp.zeros((rows_here, width), jnp.float32), jnp.zeros((), jnp.float32))
    carry = lax.fori_loop(
        0,
        blk_size - 1,
        lambda turn_index, state_now: second_visit(state_now, turn_index, True),
        carry,
    )
    travels, user_grad, scale_part = second_visit(carry, blk_size - 1, False)
    item_grad_rows = jnp.concatenate([travel[-1] for travel in travels], axis=0)
    return (user_grad, item_grad_rows, scale_part)


def body(users, items, weights, positives, log_scale):
    user_rows = users[0]
    item_rows = items[0]
    weight_rows = weights[0]
    targets = positives[0]
    rows_here = user_rows.shape[0]
    width = user_rows.shape[1]
    blk_size = lax.axis_size("blk")
    blk_index = lax.axis_index("blk")
    logit_scale = jnp.exp(log_scale[0]) / math.sqrt(width)
    total_weight = lax.psum(jnp.sum(weight_rows), ("blk", "dp"))
    user_grad, item_grad_rows, scale_part = cycle_plan(
        user_rows, item_rows, weight_rows, targets, logit_scale, blk_index, blk_size
    )
    norm = rows_here * blk_size * lax.axis_size("dp") / total_weight
    grad_users = (norm * logit_scale * user_grad).astype(jnp.bfloat16)[None]
    grad_items = (norm * logit_scale * item_grad_rows).astype(jnp.bfloat16)[None]
    scale_grad = (lax.psum(scale_part, ("blk", "dp")) / total_weight).reshape((1,))
    return (grad_users, grad_items, scale_grad)


def solution(mesh):
    placed = (P("dp", "blk", None), P("dp", "blk", None), P("dp", "blk"), P("dp", "blk"), P())
    return jax.shard_map(
        body,
        mesh=mesh,
        in_specs=placed,
        out_specs=(P("dp", "blk", None), P("dp", "blk", None), P()),
        check_vma=False,
    )
```

profile of v0, /device:TPU:1, one launch (start us, length us, event | category | flops | bytes accessed | tf_op | source)
XLA Modules:
  0.0 581.4 jit_solution(9187092153737720025)
XLA Ops:
  2.2 206.9 %while.52 = (s32[]{:T(128)}, bf16[256,512]{1,0:T(8,128)(2,1)S(1)}, f32[256]{0:T(256)S(1)}, f32[256]{0:T(256)S(1)}, f32[256]{0:T(256)S(1)}, /*index=5*/f32[256]{0...) while((s32[]{:T(128)}, bf16[256,512]{1,0:T(8,128)(2,1)S(1)}, ...), condition=%wide.region_8.9_spmd.clone, body=%wide.region_2.8_spmd.clone.sunk | while | flops 67766784 | bytes 2664917 | solution.py:92
  2.3 4.6 collective-permute-start.3
  64.3 5.0 collective-permute-start.1
  78.8 4.7 collective-permute-start.1
  93.0 4.7 collective-permute-start.1
  210.0 259.1 %while.53 = (s32[]{:T(128)}, bf16[256,512]{1,0:T(8,128)(2,1)S(1)}, f32[256]{0:T(256)S(1)}, f32[256]{0:T(256)S(1)}, f32[256,512]{1,0:T(8,128)S(1)}, /*index=5*/f3...) while((s32[]{:T(128)}, bf16[256,512]{1,0:T(8,128)(2,1)S(1)}, ...), condition=%wide.region_16.17_spmd.clone, body=%wide.region_14.16_spmd.clone.sunk | while | flops 203817232 | bytes 7634412 | solution.py:143
  211.4 5.1 collective-permute-start.7
  225.4 4.8 collective-permute-done.4
  233.6 5.0 collective-permute-start.5
  243.5 4.7 collective-permute-done.4
  260.5 4.7 collective-permute-done.4
  277.5 4.7 collective-permute-done.4
  294.5 4.7 collective-permute-done.4
  311.5 4.7 collective-permute-done.4
  328.4 4.7 collective-permute-done.4
  345.4 4.7 collective-permute-done.4
  362.4 4.7 collective-permute-done.4
  379.4 4.7 collective-permute-done.4
  396.4 4.7 collective-permute-done.4
  413.4 4.7 collective-permute-done.4
  430.4 4.7 collective-permute-done.4
  447.3 4.7 collective-permute-done.4
  464.3 4.7 collective-permute-done.4
  471.3 104.8 %all-reduce = (f32[]{:T(128)}, f32[]{:T(128)}) all-reduce(f32[]{:T(128)} %reduce_sum.109, f32[]{:T(128)S(6)} %add.259), channel_id=1, replica_groups=mesh['blk'=16,'dp'=32] {'blk','dp'}, use_global_device_ids=true, to_apply=%region_1.0 | all-reduce | flops 2 | bytes 16 | tf_op jit(solution)/shard_map/psum | solution.py:164
  (501 shorter events, 360.2 us)
Async XLA Ops:
  2.3 12.5 %collective-permute-start.3 = (f32[256]{0:T(256)S(1)}, f32[256]{0:T(256)S(1)}, u32[]{:S(2)}, u32[]{:S(2)}) collective-permute-start(f32[256]{0:T(256)S(1)} %add.344), channel_id=1, source_target_pairs={{480,0},{0,32},{32,64},{64,96},{96,128},{128,160},{160,192},{192,2... | collective-permute-start | bytes 3080 | tf_op jit(solution)/shard_map/while/body/eval_jaxpr/ppermute | solution.py:12
  72.5 13.0 %collective-permute-start.3 = (f32[256]{0:T(256)S(1)}, f32[256]{0:T(256)S(1)}, u32[]{:S(2)}, u32[]{:S(2)}) collective-permute-start(f32[256]{0:T(256)S(1)} %add.344), channel_id=1, source_target_pairs={{480,0},{0,32},{32,64},{64,96},{96,128},{128,160},{160,192},{192,2... | collective-permute-start | bytes 3080 | tf_op jit(solution)/shard_map/while/body/eval_jaxpr/ppermute | solution.py:12
  86.7 13.0 %collective-permute-start.3 = (f32[256]{0:T(256)S(1)}, f32[256]{0:T(256)S(1)}, u32[]{:S(2)}, u32[]{:S(2)}) collective-permute-start(f32[256]{0:T(256)S(1)} %add.344), channel_id=1, source_target_pairs={{480,0},{0,32},{32,64},{64,96},{96,128},{128,160},{160,192},{192,2... | collective-permute-start | bytes 3080 | tf_op jit(solution)/shard_map/while/body/eval_jaxpr/ppermute | solution.py:12
  100.9 12.3 %collective-permute-start.3 = (f32[256]{0:T(256)S(1)}, f32[256]{0:T(256)S(1)}, u32[]{:S(2)}, u32[]{:S(2)}) collective-permute-start(f32[256]{0:T(256)S(1)} %add.344), channel_id=1, source_target_pairs={{480,0},{0,32},{32,64},{64,96},{96,128},{128,160},{160,192},{192,2... | collective-permute-start | bytes 3080 | tf_op jit(solution)/shard_map/while/body/eval_jaxpr/ppermute | solution.py:12
  114.4 12.3 %collective-permute-start.3 = (f32[256]{0:T(256)S(1)}, f32[256]{0:T(256)S(1)}, u32[]{:S(2)}, u32[]{:S(2)}) collective-permute-start(f32[256]{0:T(256)S(1)} %add.344), channel_id=1, source_target_pairs={{480,0},{0,32},{32,64},{64,96},{96,128},{128,160},{160,192},{192,2... | collective-permute-start | bytes 3080 | tf_op jit(solution)/shard_map/while/body/eval_jaxpr/ppermute | solution.py:12
  128.0 12.3 %collective-permute-start.3 = (f32[256]{0:T(256)S(1)}, f32[256]{0:T(256)S(1)}, u32[]{:S(2)}, u32[]{:S(2)}) collective-permute-start(f32[256]{0:T(256)S(1)} %add.344), channel_id=1, source_target_pairs={{480,0},{0,32},{32,64},{64,96},{96,128},{128,160},{160,192},{192,2... | collective-permute-start | bytes 3080 | tf_op jit(solution)/shard_map/while/body/eval_jaxpr/ppermute | solution.py:12
  141.5 12.3 %collective-permute-start.3 = (f32[256]{0:T(256)S(1)}, f32[256]{0:T(256)S(1)}, u32[]{:S(2)}, u32[]{:S(2)}) collective-permute-start(f32[256]{0:T(256)S(1)} %add.344), channel_id=1, source_target_pairs={{480,0},{0,32},{32,64},{64,96},{96,128},{128,160},{160,192},{192,2... | collective-permute-start | bytes 3080 | tf_op jit(solution)/shard_map/while/body/eval_jaxpr/ppermute | solution.py:12
  155.1 12.3 %collective-permute-start.3 = (f32[256]{0:T(256)S(1)}, f32[256]{0:T(256)S(1)}, u32[]{:S(2)}, u32[]{:S(2)}) collective-permute-start(f32[256]{0:T(256)S(1)} %add.344), channel_id=1, source_target_pairs={{480,0},{0,32},{32,64},{64,96},{96,128},{128,160},{160,192},{192,2... | collective-permute-start | bytes 3080 | tf_op jit(solution)/shard_map/while/body/eval_jaxpr/ppermute | solution.py:12
  182.2 12.3 %collective-permute-start.3 = (f32[256]{0:T(256)S(1)}, f32[256]{0:T(256)S(1)}, u32[]{:S(2)}, u32[]{:S(2)}) collective-permute-start(f32[256]{0:T(256)S(1)} %add.344), channel_id=1, source_target_pairs={{480,0},{0,32},{32,64},{64,96},{96,128},{128,160},{160,192},{192,2... | collective-permute-start | bytes 3080 | tf_op jit(solution)/shard_map/while/body/eval_jaxpr/ppermute | solution.py:12
  211.4 18.8 %collective-permute-start.7 = (f32[256,512]{1,0:T(8,128)S(1)}, f32[256,512]{1,0:T(8,128)S(1)}, u32[]{:S(2)}, u32[]{:S(2)}) collective-permute-start(f32[256,512]{1,0:T(8,128)S(1)} %convolution_add_fusion.6), channel_id=1, source_target_pairs={{32,0},{64,32},{96,64},{128,96},{160,128},{192,160},{224,192},{256... | collective-permute-start | bytes 1572872 | tf_op jit(solution)/shard_map/while/body/eval_jaxpr/ppermute | solution.py:12
  231.7 16.6 %collective-permute-start.7 = (f32[256,512]{1,0:T(8,128)S(1)}, f32[256,512]{1,0:T(8,128)S(1)}, u32[]{:S(2)}, u32[]{:S(2)}) collective-permute-start(f32[256,512]{1,0:T(8,128)S(1)} %convolution_add_fusion.6), channel_id=1, source_target_pairs={{32,0},{64,32},{96,64},{128,96},{160,128},{192,160},{224,192},{256... | collective-permute-start | bytes 1572872 | tf_op jit(solution)/shard_map/while/body/eval_jaxpr/ppermute | solution.py:12
  249.6 15.6 %collective-permute-start.7 = (f32[256,512]{1,0:T(8,128)S(1)}, f32[256,512]{1,0:T(8,128)S(1)}, u32[]{:S(2)}, u32[]{:S(2)}) collective-permute-start(f32[256,512]{1,0:T(8,128)S(1)} %convolution_add_fusion.6), channel_id=1, source_target_pairs={{32,0},{64,32},{96,64},{128,96},{160,128},{192,160},{224,192},{256... | collective-permute-start | bytes 1572872 | tf_op jit(solution)/shard_map/while/body/eval_jaxpr/ppermute | solution.py:12
  266.6 15.6 %collective-permute-start.7 = (f32[256,512]{1,0:T(8,128)S(1)}, f32[256,512]{1,0:T(8,128)S(1)}, u32[]{:S(2)}, u32[]{:S(2)}) collective-permute-start(f32[256,512]{1,0:T(8,128)S(1)} %convolution_add_fusion.6), channel_id=1, source_target_pairs={{32,0},{64,32},{96,64},{128,96},{160,128},{192,160},{224,192},{256... | collective-permute-start | bytes 1572872 | tf_op jit(solution)/shard_map/while/body/eval_jaxpr/ppermute | solution.py:12
  283.6 15.6 %collective-permute-start.7 = (f32[256,512]{1,0:T(8,128)S(1)}, f32[256,512]{1,0:T(8,128)S(1)}, u32[]{:S(2)}, u32[]{:S(2)}) collective-permute-start(f32[256,512]{1,0:T(8,128)S(1)} %convolution_add_fusion.6), channel_id=1, source_target_pairs={{32,0},{64,32},{96,64},{128,96},{160,128},{192,160},{224,192},{256... | collective-permute-start | bytes 1572872 | tf_op jit(solution)/shard_map/while/body/eval_jaxpr/ppermute | solution.py:12
  300.6 15.6 %collective-permute-start.7 = (f32[256,512]{1,0:T(8,128)S(1)}, f32[256,512]{1,0:T(8,128)S(1)}, u32[]{:S(2)}, u32[]{:S(2)}) collective-permute-start(f32[256,512]{1,0:T(8,128)S(1)} %convolution_add_fusion.6), channel_id=1, source_target_pairs={{32,0},{64,32},{96,64},{128,96},{160,128},{192,160},{224,192},{256... | collective-permute-start | bytes 1572872 | tf_op jit(solution)/shard_map/while/body/eval_jaxpr/ppermute | solution.py:12
  317.6 15.6 %collective-permute-start.7 = (f32[256,512]{1,0:T(8,128)S(1)}, f32[256,512]{1,0:T(8,128)S(1)}, u32[]{:S(2)}, u32[]{:S(2)}) collective-permute-start(f32[256,512]{1,0:T(8,128)S(1)} %convolution_add_fusion.6), channel_id=1, source_target_pairs={{32,0},{64,32},{96,64},{128,96},{160,128},{192,160},{224,192},{256... | collective-permute-start | bytes 1572872 | tf_op jit(solution)/shard_map/while/body/eval_jaxpr/ppermute | solution.py:12
  334.6 15.6 %collective-permute-start.7 = (f32[256,512]{1,0:T(8,128)S(1)}, f32[256,512]{1,0:T(8,128)S(1)}, u32[]{:S(2)}, u32[]{:S(2)}) collective-permute-start(f32[256,512]{1,0:T(8,128)S(1)} %convolution_add_fusion.6), channel_id=1, source_target_pairs={{32,0},{64,32},{96,64},{128,96},{160,128},{192,160},{224,192},{256... | collective-permute-start | bytes 1572872 | tf_op jit(solution)/shard_map/while/body/eval_jaxpr/ppermute | solution.py:12
  351.6 15.6 %collective-permute-start.7 = (f32[256,512]{1,0:T(8,128)S(1)}, f32[256,512]{1,0:T(8,128)S(1)}, u32[]{:S(2)}, u32[]{:S(2)}) collective-permute-start(f32[256,512]{1,0:T(8,128)S(1)} %convolution_add_fusion.6), channel_id=1, source_target_pairs={{32,0},{64,32},{96,64},{128,96},{160,128},{192,160},{224,192},{256... | collective-permute-start | bytes 1572872 | tf_op jit(solution)/shard_map/while/body/eval_jaxpr/ppermute | solution.py:12
  368.5 15.6 %collective-permute-start.7 = (f32[256,512]{1,0:T(8,128)S(1)}, f32[256,512]{1,0:T(8,128)S(1)}, u32[]{:S(2)}, u32[]{:S(2)}) collective-permute-start(f32[256,512]{1,0:T(8,128)S(1)} %convolution_add_fusion.6), channel_id=1, source_target_pairs={{32,0},{64,32},{96,64},{128,96},{160,128},{192,160},{224,192},{256... | collective-permute-start | bytes 1572872 | tf_op jit(solution)/shard_map/while/body/eval_jaxpr/ppermute | solution.py:12
  385.5 15.6 %collective-permute-start.7 = (f32[256,512]{1,0:T(8,128)S(1)}, f32[256,512]{1,0:T(8,128)S(1)}, u32[]{:S(2)}, u32[]{:S(2)}) collective-permute-start(f32[256,512]{1,0:T(8,128)S(1)} %convolution_add_fusion.6), channel_id=1, source_target_pairs={{32,0},{64,32},{96,64},{128,96},{160,128},{192,160},{224,192},{256... | collective-permute-start | bytes 1572872 | tf_op jit(solution)/shard_map/while/body/eval_jaxpr/ppermute | solution.py:12
  402.5 15.6 %collective-permute-start.7 = (f32[256,512]{1,0:T(8,128)S(1)}, f32[256,512]{1,0:T(8,128)S(1)}, u32[]{:S(2)}, u32[]{:S(2)}) collective-permute-start(f32[256,512]{1,0:T(8,128)S(1)} %convolution_add_fusion.6), channel_id=1, source_target_pairs={{32,0},{64,32},{96,64},{128,96},{160,128},{192,160},{224,192},{256... | collective-permute-start | bytes 1572872 | tf_op jit(solution)/shard_map/while/body/eval_jaxpr/ppermute | solution.py:12
  419.5 15.6 %collective-permute-start.7 = (f32[256,512]{1,0:T(8,128)S(1)}, f32[256,512]{1,0:T(8,128)S(1)}, u32[]{:S(2)}, u32[]{:S(2)}) collective-permute-start(f32[256,512]{1,0:T(8,128)S(1)} %convolution_add_fusion.6), channel_id=1, source_target_pairs={{32,0},{64,32},{96,64},{128,96},{160,128},{192,160},{224,192},{256... | collective-permute-start | bytes 1572872 | tf_op jit(solution)/shard_map/while/body/eval_jaxpr/ppermute | solution.py:12
  436.5 15.6 %collective-permute-start.7 = (f32[256,512]{1,0:T(8,128)S(1)}, f32[256,512]{1,0:T(8,128)S(1)}, u32[]{:S(2)}, u32[]{:S(2)}) collective-permute-start(f32[256,512]{1,0:T(8,128)S(1)} %convolution_add_fusion.6), channel_id=1, source_target_pairs={{32,0},{64,32},{96,64},{128,96},{160,128},{192,160},{224,192},{256... | collective-permute-start | bytes 1572872 | tf_op jit(solution)/shard_map/while/body/eval_jaxpr/ppermute | solution.py:12
  453.5 15.6 %collective-permute-start.7 = (f32[256,512]{1,0:T(8,128)S(1)}, f32[256,512]{1,0:T(8,128)S(1)}, u32[]{:S(2)}, u32[]{:S(2)}) collective-permute-start(f32[256,512]{1,0:T(8,128)S(1)} %convolution_add_fusion.6), channel_id=1, source_target_pairs={{32,0},{64,32},{96,64},{128,96},{160,128},{192,160},{224,192},{256... | collective-permute-start | bytes 1572872 | tf_op jit(solution)/shard_map/while/body/eval_jaxpr/ppermute | solution.py:12
  (100 other events, 698.8 us)
where the time goes:
time: 585 us; the launch traced here: 581 us
  starting transfers between devices  322 us (55%)
  blocking collectives  105 us (18%)
  waiting for transfers between devices  96.2 us (16%)
  matrix products  33.8 us (6%)
  loops' own time  11 us (2%)
  other arithmetic  6.9 us (1%)
    ppermute x120, starting transfers between devices, shifted(): return lax.ppermute(block, axis, route)  322 us
    psum x1, blocking collectives, body(): total_weight = lax.psum(jnp.sum(weight_rows), ('blk', 'dp'))  105 us
    ppermute x120, waiting for transfers between devices, shifted(): return lax.ppermute(block, axis, route)  96.2 us
    dot_general x32, matrix products, block_scores(): jnp.einsum('rd,cd->rc', user_rows, item_block, preferred_element_type=jnp...  20.6 us
  transfers between devices with their start and end apart: 120, of which 48 were waited for; matrix products, arithmetic and copies ran while one was open for 2% of the time, Pallas kernels for 0%

commit v1 on v0

v1 whole, which is shorter than its diff:
```python
import functools
import math

import jax
import jax.numpy as jnp
from jax import lax
from jax.experimental import pallas as pl
from jax.experimental.pallas import tpu as pltpu
from jax.sharding import PartitionSpec as P

MESH = pl.DeviceIdType.MESH
F32 = jnp.float32
BF16 = jnp.bfloat16
LOW = -3.0e38
CHUNK = 32

(
    U_RIGHT_0, U_LEFT_1, U_RIGHT_1, U_LEFT_0, U_RELAY_RIGHT, U_RELAY_LEFT,
    I_CORE, I_Y_0, I_Y_1, I_PASS_0, I_PASS_1,
    WP_1, WP_2, WP_3, CW_1, CW_2, CW_3, RS_1, RS_2, RS_3, CS_1, CS_2, CS_3,
    GU_FAR_RIGHT, GU_FAR_LEFT, GU_RIGHT_0, GU_RIGHT_1, GU_LEFT_0, GU_LEFT_1,
    GI_CORE_0, GI_CORE_1, GI_Y,
    TRANSFERS,
) = range(33)


def dot_nt(a, b):
    return lax.dot_general(a, b, (((1,), (1,)), ((), ())), preferred_element_type=F32)


def dot_tn(a, b):
    return lax.dot_general(a, b, (((0,), (0,)), ((), ())), preferred_element_type=F32)


def fold_rows(block, op):
    total = block[0:8]
    for r in range(8, block.shape[0], 8):
        total = op(total, block[r : r + 8])
    return total


def kernel(
    nx, nyc, n_dp, n_blk,
    users, items, weights, positives, log_scale,
    gu_out, gi_out, scale_out,
    u_all, i_all, wp, t_all, g_all, wcol, pcol, acol, row_m, row_s,
    rowst, colst, cwst, brow,
    far, far_right, far_left, to_left, to_right, from_left, from_right,
    own_gu, own_gi, other_gi, core_0, core_1, got_core_0, got_core_1, to_y, from_y,
    red_dp, red_blk,
    local_sem, send, recv, dp_send, dp_recv, blk_send, blk_recv,
):
    n = users.shape[0]
    width = users.shape[1]
    half = n // 2
    cols = nyc * n
    me = lax.axis_index("blk")
    my_dp = lax.axis_index("dp")
    x = me // nyc
    yc = me % nyc
    core = yc % 2
    y = yc // 2

    def at_x(d):
        return {"blk": ((x + d) % nx) * nyc + yc, "dp": my_dp}

    def at_yc(d):
        c = 1 - core if d % 2 else core
        w = 1 - y if d // 2 else y
        return {"blk": x * nyc + w * 2 + c, "dp": my_dp}

    right, left = at_x(1), at_x(nx - 1)

    def remote(src, dst, number, device):
        return pltpu.make_async_remote_copy(
            src_ref=src, dst_ref=dst, send_sem=send.at[number], recv_sem=recv.at[number],
            device_id=device, device_id_type=MESH,
        )

    own_users = pltpu.make_async_copy(users, u_all.at[pl.ds(0, n)], local_sem.at[0])
    own_items = pltpu.make_async_copy(items, i_all.at[pl.ds(0, n)], local_sem.at[1])
    own_users.start()
    own_items.start()

    barrier = pltpu.get_barrier_semaphore()

    def greet_blk(d, carry):
        pl.semaphore_signal(
            barrier, inc=1, device_id={"blk": (me + d) % n_blk, "dp": my_dp}, device_id_type=MESH
        )
        return carry

    def greet_dp(d, carry):
        pl.semaphore_signal(
            barrier, inc=1, device_id={"blk": me, "dp": (my_dp + d) % n_dp}, device_id_type=MESH
        )
        return carry

    lax.fori_loop(1, n_blk, greet_blk, 0)
    lax.fori_loop(1, n_dp, greet_dp, 0)
    wp[0] = jnp.zeros((8, n), F32)
    wp[0, 0:1, :] = weights[...]
    wp[0, 1:2, :] = positives[...].astype(F32)
    own_users.wait()
    own_items.wait()
    pl.semaphore_wait(barrier, n_blk + n_dp - 2)

    def u_rows(slot, h):
        return u_all.at[pl.ds(slot * n + h * half, half)]

    def i_rows(slot, h):
        return i_all.at[pl.ds(slot * n + h * half, half)]

    started = []

    def start(copy):
        copy.start()
        started.append(copy)
        return copy

    wp_copies = [start(remote(wp.at[0], wp.at[d], WP_1 + d - 1, at_x(d))) for d in (1, 2, 3)]
    u_r0 = start(remote(u_rows(0, 0), u_rows(1, 0), U_RIGHT_0, right))
    u_l1 = start(remote(u_rows(0, 1), u_rows(3, 1), U_LEFT_1, left))
    i_core = start(remote(i_all.at[pl.ds(0, n)], i_all.at[pl.ds(n, n)], I_CORE, at_yc(1)))
    i_y0 = start(remote(i_rows(0, 0), i_rows(2, 0), I_Y_0, at_yc(2)))
    u_r1 = start(remote(u_rows(0, 1), u_rows(1, 1), U_RIGHT_1, right))
    u_l0 = start(remote(u_rows(0, 0), u_rows(3, 0), U_LEFT_0, left))
    i_y1 = start(remote(i_rows(0, 1), i_rows(2, 1), I_Y_1, at_yc(2)))

    k = jnp.exp(jnp.full((1, 2 * n), log_scale[0], F32)) * (1.0 / (math.sqrt(width) * math.log(2.0)))

    def scores(slot, h):
        block = dot_nt(u_all[slot * n : (slot + 1) * n, :], i_all[h * 2 * n : (h + 1) * 2 * n, :])
        t_all[slot * n : (slot + 1) * n, h * 2 * n : (h + 1) * 2 * n] = block * k

    lane = lax.broadcasted_iota(jnp.int32, (1, 128), 1)

    def column_ids(c):
        block, part = c // (n // 128), c % (n // 128)
        owner = at_yc(block)["blk"]
        return (owner * n + part * 128 + lane).astype(F32)

    chunks = cols // 128
    ids = [column_ids(c) for c in range(chunks)]

    for c in wp_copies:
        c.wait_recv()
    for slot in range(nx):
        wcol[slot * n : (slot + 1) * n, :] = jnp.broadcast_to(wp[slot, 0:1, :], (128, n)).T
        pcol[slot * n : (slot + 1) * n, :] = jnp.broadcast_to(wp[slot, 1:2, :], (128, n)).T

    def weigh(i, total):
        rows = pl.ds(pl.multiple_of(i * CHUNK, CHUNK), CHUNK)
        w = wcol[rows, :]
        p = pcol[rows, :]
        return tuple(
            total[c] + fold_rows(jnp.where(p == ids[c], w, 0.0), jnp.add) for c in range(chunks)
        )

    total = lax.fori_loop(
        0, nx * n // CHUNK, weigh, tuple(jnp.zeros((8, 128), F32) for _ in range(chunks))
    )
    cwst[0] = jnp.zeros((8, n), F32)
    per = n // 128
    for c in range(chunks):
        cwst[0, c // per : c // per + 1, (c % per) * 128 : (c % per + 1) * 128] = jnp.sum(
            total[c], axis=0, keepdims=True
        )
    cw_copies = [start(remote(cwst.at[0], cwst.at[d], CW_1 + d - 1, at_yc(d))) for d in (1, 2, 3)]

    i_core.wait_recv()
    scores(0, 0)
    u_r0.wait_recv()
    relay_r = start(remote(u_rows(1, 0), u_rows(2, 0), U_RELAY_RIGHT, right))
    u_l1.wait_recv()
    relay_l = start(remote(u_rows(3, 1), u_rows(2, 1), U_RELAY_LEFT, left))
    i_y0.wait_recv()
    i_p0 = start(remote(i_rows(2, 0), i_rows(3, 0), I_PASS_0, at_yc(1)))
    u_r1.wait_recv()
    i_y1.wait_recv()
    i_p1 = start(remote(i_rows(2, 1), i_rows(3, 1), I_PASS_1, at_yc(1)))
    scores(1, 0)
    u_l0.wait_recv()
    scores(3, 0)
    i_p0.wait_recv()
    i_p1.wait_recv()

    def statistics(slot):
        def maxima(i, best):
            rows = pl.ds(pl.multiple_of(slot * n + i * CHUNK, CHUNK), CHUNK)
            top = None
            out = []
            for c in range(chunks):
                t = t_all[rows, c * 128 : (c + 1) * 128]
                top = t if top is None else jnp.maximum(top, t)
                out.append(jnp.maximum(best[c], fold_rows(t, jnp.maximum)))
            here = pl.ds(pl.multiple_of(i * CHUNK, CHUNK), CHUNK)
            row_m[here, :] = jnp.broadcast_to(jnp.max(top, axis=1, keepdims=True), (CHUNK, 128))
            return tuple(out)

        best = lax.fori_loop(
            0, n // CHUNK, maxima, tuple(jnp.full((8, 128), LOW, F32) for _ in range(chunks))
        )
        best = [jnp.max(b, axis=0, keepdims=True) for b in best]

        def sums(i, total):
            rows = pl.ds(pl.multiple_of(slot * n + i * CHUNK, CHUNK), CHUNK)
            here = pl.ds(pl.multiple_of(i * CHUNK, CHUNK), CHUNK)
            m = row_m[here, :]
            line = None
            out = []
            for c in range(chunks):
                t = t_all[rows, c * 128 : (c + 1) * 128]
                e = jnp.exp2(t - m)
                line = e if line is None else line + e
                out.append(total[c] + fold_rows(jnp.exp2(t - best[c]), jnp.add))
            row_s[here, :] = jnp.broadcast_to(jnp.sum(line, axis=1, keepdims=True), (CHUNK, 128))
            return tuple(out)

        total = lax.fori_loop(
            0, n // CHUNK, sums, tuple(jnp.zeros((8, 128), F32) for _ in range(chunks))
        )
        total = [jnp.sum(b, axis=0, keepdims=True) for b in total]
        first = lax.broadcasted_iota(jnp.int32, (n, 128), 1) == 0
        packed = jnp.where(first, row_m[...], row_s[...]).T
        rowst[0, slot : slot + 1, :] = packed[0:1, :]
        rowst[0, nx + slot : nx + slot + 1, :] = packed[1:2, :]
        return best, total

    parts = {}
    for slot in (0, 1, 3):
        scores(slot, 1)
        parts[slot] = statistics(slot)
    relay_r.wait_recv()
    relay_l.wait_recv()
    scores(2, 0)
    scores(2, 1)
    parts[2] = statistics(2)

    for c in range(chunks):
        m = functools.reduce(jnp.maximum, [parts[s][0][c] for s in range(nx)])
        l = sum(parts[s][1][c] * jnp.exp2(parts[s][0][c] - m) for s in range(nx))
        b, q = c // per, (c % per) * 128
        colst[0, b : b + 1, q : q + 128] = m
        colst[0, nyc + b : nyc + b + 1, q : q + 128] = l

    rs_copies = [start(remote(rowst.at[0], rowst.at[d], RS_1 + d - 1, at_x(d))) for d in (1, 2, 3)]
    cs_copies = [start(remote(colst.at[0], colst.at[d], CS_1 + d - 1, at_yc(d))) for d in (1, 2, 3)]
    for c in cw_copies + cs_copies:
        c.wait_recv()
    for b in range(nyc):
        ms = [colst[d, b ^ d : (b ^ d) + 1, :] for d in range(nyc)]
        ls = [colst[d, nyc + (b ^ d) : nyc + (b ^ d) + 1, :] for d in range(nyc)]
        w = sum(cwst[d, b ^ d : (b ^ d) + 1, :] for d in range(nyc))
        m = functools.reduce(jnp.maximum, ms)
        l = sum(li * jnp.exp2(mi - m) for mi, li in zip(ms, ls))
        brow[0:1, b * n : (b + 1) * n] = m + jnp.log2(l / w)
    for c in rs_copies:
        c.wait_recv()
    for r in range(nx):
        at = [(r - d) % nx for d in range(nx)]
        ms = [rowst[d, at[d] : at[d] + 1, :] for d in range(nx)]
        ls = [rowst[d, nx + at[d] : nx + at[d] + 1, :] for d in range(nx)]
        m = functools.reduce(jnp.maximum, ms)
        l = sum(li * jnp.exp2(mi - m) for mi, li in zip(ms, ls))
        a = m + jnp.log2(l / wp[r, 0:1, :])
        acol[r * n : (r + 1) * n, :] = jnp.broadcast_to(a, (128, n)).T

    b_rows = [brow[0:1, c * 128 : (c + 1) * 128] for c in range(chunks)]

    def gradients(slot, part):
        def step(i, part):
            rows = pl.ds(pl.multiple_of(slot * n + i * CHUNK, CHUNK), CHUNK)
            a = acol[rows, :]
            w2 = 2.0 * wcol[rows, :]
            p = pcol[rows, :]
            for c in range(chunks):
                t = t_all[rows, c * 128 : (c + 1) * 128]
                g = jnp.exp2(t - a) + jnp.exp2(t - b_rows[c])
                g = g - jnp.where(p == ids[c], w2, 0.0)
                part = part + fold_rows(g * t, jnp.add)
                g_all[rows, c * 128 : (c + 1) * 128] = g.astype(BF16)
            return part

        return lax.fori_loop(0, n // CHUNK, step, part)

    def user_part(slot):
        return jnp.dot(
            g_all[slot * n : (slot + 1) * n, :], i_all[...], preferred_element_type=F32
        )

    def item_part(slot):
        return dot_tn(g_all[:, slot * n : (slot + 1) * n], u_all[...])

    part = gradients(2, jnp.zeros((8, 128), F32))
    far[...] = user_part(2).astype(BF16)
    gu_fr = start(remote(far.at[pl.ds(0, half)], far_right, GU_FAR_RIGHT, right))
    gu_fl = start(remote(far.at[pl.ds(half, half)], far_left, GU_FAR_LEFT, left))
    part = gradients(1, part)
    own_gu[...] = user_part(1)
    to_left[0:half, :] = own_gu[0:half, :].astype(BF16)
    gu_l0 = start(remote(to_left.at[pl.ds(0, half)], from_right.at[pl.ds(0, half)], GU_LEFT_0, left))
    part = gradients(3, part)
    own_gi[...] = user_part(3)
    to_right[half:n, :] = own_gi[half:n, :].astype(BF16)
    gu_r1 = start(
        remote(to_right.at[pl.ds(half, half)], from_left.at[pl.ds(half, half)], GU_RIGHT_1, right)
    )
    part = gradients(0, part)

    red_dp[0] = jnp.zeros((8, 128), F32)
    red_dp[0, 0:1, :] = jnp.broadcast_to(jnp.sum(part, keepdims=True) * math.log(2.0), (1, 128))
    red_dp[0, 1:2, :] = jnp.broadcast_to(jnp.sum(wp[0, 0:1, :], keepdims=True), (1, 128))

    def dp_copy(d):
        return pltpu.make_async_remote_copy(
            src_ref=red_dp.at[0], dst_ref=red_dp.at[d], send_sem=dp_send.at[d], recv_sem=dp_recv.at[d],
            device_id={"blk": me, "dp": (my_dp + d) % n_dp}, device_id_type=MESH,
        )

    def blk_copy(d):
        return pltpu.make_async_remote_copy(
            src_ref=red_blk.at[0], dst_ref=red_blk.at[d], send_sem=blk_send.at[d], recv_sem=blk_recv.at[d],
            device_id={"blk": (me + d) % n_blk, "dp": my_dp}, device_id_type=MESH,
        )

    def each(first, last, copy, action):
        def step(d, carry):
            action(copy(d))
            return carry

        lax.fori_loop(first, last, step, 0)

    each(1, n_dp, dp_copy, lambda c: c.start())

    core_0[...] = item_part(1).astype(BF16)
    gi_c0 = start(remote(core_0, got_core_0, GI_CORE_0, at_yc(1)))
    core_1[...] = item_part(3).astype(BF16)
    gi_c1 = start(remote(core_1, got_core_1, GI_CORE_1, at_yc(1)))

    gu_fr.wait_recv()
    to_right[0:half, :] = (own_gi[0:half, :] + far_right[...].astype(F32)).astype(BF16)
    gu_r0 = start(
        remote(to_right.at[pl.ds(0, half)], from_left.at[pl.ds(0, half)], GU_RIGHT_0, right)
    )
    gu_fl.wait_recv()
    to_left[half:n, :] = (own_gu[half:n, :] + far_left[...].astype(F32)).astype(BF16)
    gu_l1 = start(
        remote(to_left.at[pl.ds(half, half)], from_right.at[pl.ds(half, half)], GU_LEFT_1, left)
    )
    other_gi[...] = item_part(2)
    gi_c1.wait_recv()
    to_y[...] = (other_gi[...] + got_core_1[...].astype(F32)).astype(BF16)
    gi_y = start(remote(to_y, from_y, GI_Y, at_yc(2)))

    each(1, n_dp, dp_copy, lambda c: c.wait_recv())
    red_blk[0] = jnp.sum(red_dp[...], axis=0)
    each(1, n_blk, blk_copy, lambda c: c.start())

    own_gu[...] = user_part(0)
    own_gi[...] = item_part(0)
    gi_c0.wait_recv()
    own_gi[...] = own_gi[...] + got_core_0[...].astype(F32)

    each(1, n_blk, blk_copy, lambda c: c.wait_recv())
    sums = jnp.sum(red_blk[...], axis=0)
    weight = sums[1:2, :]
    scale_out[0] = (sums[0:1, :] / weight)[0, 0]
    rows_total = float(n * n_blk * n_dp)
    factor = (rows_total / weight) * (k[:, 0:128] * math.log(2.0))
    factor = jnp.concatenate([factor] * (width // 128), axis=1)

    gu_l0.wait_recv()
    gu_r1.wait_recv()
    gu_r0.wait_recv()
    gu_l1.wait_recv()
    gu_out[...] = (
        factor * (own_gu[...] + from_left[...].astype(F32) + from_right[...].astype(F32))
    ).astype(BF16)
    gi_y.wait_recv()
    gi_out[...] = (factor * (own_gi[...] + from_y[...].astype(F32))).astype(BF16)

    for c in started:
        c.wait_send()
    each(1, n_dp, dp_copy, lambda c: c.wait_send())
    each(1, n_blk, blk_copy, lambda c: c.wait_send())


def body(users, items, weights, positives, log_scale):
    users, items = users[0], items[0]
    n, width = users.shape
    n_blk, n_dp = lax.axis_size("blk"), lax.axis_size("dp")
    nyc = 4
    nx = n_blk // nyc
    any_space = pl.BlockSpec(memory_space=pl.ANY)
    vmem = pl.BlockSpec(memory_space=pltpu.VMEM)
    smem = pl.BlockSpec(memory_space=pltpu.SMEM)
    V = pltpu.VMEM
    rows, cols = nx * n, nyc * n
    half = n // 2
    gu, gi, scale = pl.pallas_call(
        functools.partial(kernel, nx, nyc, n_dp, n_blk),
        out_shape=(
            jax.ShapeDtypeStruct((n, width), BF16),
            jax.ShapeDtypeStruct((n, width), BF16),
            jax.ShapeDtypeStruct((1,), F32),
        ),
        in_specs=[any_space, any_space, vmem, vmem, smem],
        out_specs=(vmem, vmem, smem),
        scratch_shapes=[
            V((rows, width), BF16),
            V((cols, width), BF16),
            V((nx, 8, n), F32),
            V((rows, cols), F32),
            V((rows, cols), BF16),
            V((rows, 128), F32),
            V((rows, 128), F32),
            V((rows, 128), F32),
            V((n, 128), F32),
            V((n, 128), F32),
            V((nx, 8, n), F32),
            V((nyc, 8, n), F32),
            V((nyc, 8, n), F32),
            V((8, cols), F32),
            V((n, width), BF16),
            V((half, width), BF16),
            V((half, width), BF16),
            V((n, width), BF16),
            V((n, width), BF16),
            V((n, width), BF16),
            V((n, width), BF16),
            V((n, width), F32),
            V((n, width), F32),
            V((n, width), F32),
            V((n, width), BF16),
            V((n, width), BF16),
            V((n, width), BF16),
            V((n, width), BF16),
            V((n, width), BF16),
            V((n, width), BF16),
            V((n_dp, 8, 128), F32),
            V((n_blk, 8, 128), F32),
            pltpu.SemaphoreType.DMA((2,)),
            pltpu.SemaphoreType.DMA((TRANSFERS,)),
            pltpu.SemaphoreType.DMA((TRANSFERS,)),
            pltpu.SemaphoreType.DMA((n_dp,)),
            pltpu.SemaphoreType.DMA((n_dp,)),
            pltpu.SemaphoreType.DMA((n_blk,)),
            pltpu.SemaphoreType.DMA((n_blk,)),
        ],
        compiler_params=pltpu.CompilerParams(
            collective_id=0, has_side_effects=True, vmem_limit_bytes=48 * 1024 * 1024
        ),
        cost_estimate=pl.CostEstimate(
            flops=6 * rows * cols * width, bytes_accessed=4 * n * width * 2,
            transcendentals=4 * rows * cols,
        ),
        name="loss_gradients",
    )(users, items, weights, positives, log_scale)
    return gu[None], gi[None], scale


def solution(mesh):
    placed = (P("dp", "blk", None), P("dp", "blk", None), P("dp", "blk"), P("dp", "blk"), P())
    return jax.shard_map(
        body,
        mesh=mesh,
        in_specs=placed,
        out_specs=(P("dp", "blk", None), P("dp", "blk", None), P()),
        check_vma=False,
    )
```

time: 585 us -> 67.8 us (0.12)
  starting transfers between devices: 322 us -> 0 us
  blocking collectives: 105 us -> 0 us
  waiting for transfers between devices: 96.2 us -> 0 us
  Pallas kernels: 0 us -> 60.5 us
  matrix products: 33.8 us -> 0 us
  loops' own time: 11 us -> 0 us
  other arithmetic: 6.9 us -> 0 us
    ppermute x120 -> x0, starting transfers between devices: 322 us -> none  [shifted(): return lax.ppermute(block, axis, route)]
    psum x1 -> x0, blocking collectives: 105 us -> none  [body(): total_weight = lax.psum(jnp.sum(weight_rows), ('blk', 'dp'))]
    ppermute x120 -> x0, waiting for transfers between devices: 96.2 us -> none  [shifted(): return lax.ppermute(block, axis, route)]
    pallas_call x0 -> x1, Pallas kernels: none -> 60.5 us  [body(): pl.pallas_call(functools.partial(kernel, nx, nyc, n_dp, n_blk), out_shape...]
    dot_general x64 -> x0, matrix products: 33.8 us -> none  [the longest x32 20.6 us: block_scores(): jnp.einsum('rd,cd->rc', user_rows, item_block, preferred_element_type=jnp...]
    another operation x2 -> x0, loops' own time: 11 us -> none  [the longest x1 9.71 us: cycle_plan(): lax.fori_loop(0, blk_size - 1, lambda turn_index, state_now: second_visit...]
    reduce_sum x33 -> x0, other arithmetic: 6.15 us -> none  [the longest x16 3.13 us: first_visit(): jnp.sum(jnp.exp(scores - new_max[:, None]), axis=1)]
  transfers between devices with their start and end apart: 120 -> 0, of which waited for: 48 -> 0; matrix products, arithmetic and copies ran while one was open for 2% -> 0% of each run, Pallas kernels for 0% -> 0%
where the time goes in v1:
time: 67.8 us; the launch traced here: 67.5 us
  Pallas kernels  60.5 us (89%)
  local copies, waits for them, and re-layouts  3.99 us (6%)
  between operations  3.05 us (4%)
    pallas_call x1, Pallas kernels, body(): pl.pallas_call(functools.partial(kernel, nx, nyc, n_dp, n_blk), out_shape...  60.5 us
    unnamed x10, local copies, waits for them, and re-layouts  3.99 us

profile of v1, /device:TPU:1, one launch (start us, length us, event | category | flops | bytes accessed | tf_op | source)
XLA Modules:
  0.0 67.5 jit_solution(10462978275726859388)
XLA Ops:
  1.3 0.0 copy-start.3
  1.3 0.0 copy-start.2
  1.3 0.7 copy-done.3
  2.0 0.0 copy-done.2
  2.0 0.0 copy-start
  2.0 0.9 %copy-done = bf16[1,256,512]{2,1,0:T(8,128)(2,1)S(1)} copy-done((bf16[1,256,512]{2,1,0:T(8,128)(2,1)S(1)}, bf16[1,256,512]{2,1,0:T(8,128)(2,1)}, u32[]{:S(2)}) %copy-start) | copy-done | bytes 262168
  2.9 0.0 copy-start.1
  2.9 0.9 %copy-done.1 = bf16[1,256,512]{2,1,0:T(8,128)(2,1)S(1)} copy-done((bf16[1,256,512]{2,1,0:T(8,128)(2,1)S(1)}, bf16[1,256,512]{2,1,0:T(8,128)(2,1)}, u32[]{:S(2)}) %copy-start.1) | copy-done | bytes 262168
  3.9 60.5 %loss_gradients.1 = (bf16[256,512]{1,0:T(8,128)(2,1)S(1)}, bf16[256,512]{1,0:T(8,128)(2,1)S(1)}, f32[1]{0:T(128)}) custom-call(bf16[256,512]{1,0:T(8,128)(2,1)S(1)} %bitcast.6, bf16[256,512]{1,0:T(8,128)(2,1)S(1)} %bitcast.7, f32[1,256]{1,0:T(1,128)S(1)} %copy-done.2, s32[1,256]{1,0:T(1,128)S(1)} %copy-done.3, f32[1]{0:T(128)S(6)} %copy.11.log_scale), custom_call_target="tpu_custom_call" | custom-call | flops 3221225472 | bytes 1048576 | tf_op jit(solution)/shard_map/loss_gradients/pallas_call | solution.py:401
  64.4 0.7 %copy.12 = bf16[1,256,512]{2,1,0:T(8,128)(2,1)} copy(bf16[1,256,512]{2,1,0:T(8,128)(2,1)S(1)} %bitcast.5) | data formatting | bytes 524288
  65.1 0.7 %copy.13 = bf16[1,256,512]{2,1,0:T(8,128)(2,1)} copy(bf16[1,256,512]{2,1,0:T(8,128)(2,1)S(1)} %bitcast.4) | data formatting | bytes 524288
Async XLA Ops:
  1.3 0.7 %copy-start.3 = (s32[1,256]{1,0:T(1,128)S(1)}, s32[1,256]{1,0:T(1,128)}, u32[]{:S(2)}) copy-start(s32[1,256]{1,0:T(1,128)} %positives.1) | copy-start | bytes 3076
  1.3 0.7 %copy-start.2 = (f32[1,256]{1,0:T(1,128)S(1)}, f32[1,256]{1,0:T(1,128)}, u32[]{:S(2)}) copy-start(f32[1,256]{1,0:T(1,128)} %weights.1) | copy-start | bytes 3076
  2.0 0.9 %copy-start = (bf16[1,256,512]{2,1,0:T(8,128)(2,1)S(1)}, bf16[1,256,512]{2,1,0:T(8,128)(2,1)}, u32[]{:S(2)}) copy-start(bf16[1,256,512]{2,1,0:T(8,128)(2,1)} %param.5) | copy-start | bytes 786436
  2.9 0.9 %copy-start.1 = (bf16[1,256,512]{2,1,0:T(8,128)(2,1)S(1)}, bf16[1,256,512]{2,1,0:T(8,128)(2,1)}, u32[]{:S(2)}) copy-start(bf16[1,256,512]{2,1,0:T(8,128)(2,1)} %param.6) | copy-start | bytes 786436

commit v2 on v1

v2 whole, which is shorter than its diff:
```python
import functools
import math

import jax
import jax.numpy as jnp
from jax import lax
from jax.experimental import pallas as pl
from jax.experimental.pallas import tpu as pltpu
from jax.sharding import PartitionSpec as P

MESH = pl.DeviceIdType.MESH
F32 = jnp.float32
BF16 = jnp.bfloat16
LOW = -3.0e38
CHUNK = 32

(
    U_RIGHT_0, U_LEFT_1, U_RIGHT_1, U_LEFT_0, U_RELAY_RIGHT, U_RELAY_LEFT,
    I_CORE, I_Y_0, I_Y_1, I_PASS_0, I_PASS_1,
    WP_RIGHT, WP_LEFT, WP_RELAY, RS_1, RS_2, RS_3, CS_1, CS_2, CS_3,
    GU_FAR_RIGHT, GU_FAR_LEFT, GU_RIGHT_0, GU_RIGHT_1, GU_LEFT_0, GU_LEFT_1,
    GI_CORE_0, GI_CORE_1, GI_Y,
    TRANSFERS,
) = range(30)


def dot_nt(a, b):
    return lax.dot_general(a, b, (((1,), (1,)), ((), ())), preferred_element_type=F32)


def dot_tn(a, b):
    return lax.dot_general(a, b, (((0,), (0,)), ((), ())), preferred_element_type=F32)


def fold_rows(block, op):
    total = block[0:8]
    for r in range(8, block.shape[0], 8):
        total = op(total, block[r : r + 8])
    return total


def kernel(
    nx, nyc, n_dp, n_blk,
    users, items, weights, positives, log_scale,
    gu_out, gi_out, scale_out,
    u_all, i_all, w_in, p_in, wp, t_all, g_all, wcol, pcol, acol, row_m, lines,
    rowst, colst, brow,
    far, far_right, far_left, to_left, to_right, from_left, from_right,
    own_gu, own_gi, other_gi, core_0, core_1, got_core_0, got_core_1, to_y, from_y,
    red_dp, red_blk,
    local_sem, send, recv, dp_send, dp_recv, blk_send, blk_recv, hello,
):
    n = users.shape[0]
    width = users.shape[1]
    half = n // 2
    cols = nyc * n
    chunks = cols // 128
    per = n // 128
    steps = n // CHUNK
    me = lax.axis_index("blk")
    my_dp = lax.axis_index("dp")
    x = me // nyc
    yc = me % nyc
    core = yc % 2
    y = yc // 2
    depth = n_dp // 2
    rank = (my_dp % depth) * 2 + my_dp // depth

    def at_x(d):
        return {"blk": ((x + d) % nx) * nyc + yc, "dp": my_dp}

    def at_yc(d):
        c = 1 - core if d % 2 else core
        w = 1 - y if d // 2 else y
        return {"blk": x * nyc + w * 2 + c, "dp": my_dp}

    def at_rank(r):
        return {"blk": me, "dp": (r % 2) * depth + r // 2}

    right, left = at_x(1), at_x(nx - 1)

    def remote(src, dst, number, device):
        return pltpu.make_async_remote_copy(
            src_ref=src, dst_ref=dst, send_sem=send.at[number], recv_sem=recv.at[number],
            device_id=device, device_id_type=MESH,
        )

    def loop(first, last, action):
        def step(d, carry):
            action(d)
            return carry

        lax.fori_loop(first, last, step, 0)

    def greet(semaphore, device):
        pl.semaphore_signal(semaphore, inc=1, device_id=device, device_id_type=MESH)

    barrier = pltpu.get_barrier_semaphore()
    for device in (right, left, at_yc(1), at_yc(2)):
        greet(barrier, device)
    locals_ = [
        pltpu.make_async_copy(src, dst, local_sem.at[i])
        for i, (src, dst) in enumerate(
            [
                (users, u_all.at[pl.ds(0, n)]),
                (items, i_all.at[pl.ds(0, n)]),
                (weights, w_in),
                (positives, p_in),
            ]
        )
    ]
    for c in locals_:
        c.start()
    loop(rank + 1, n_dp, lambda r: greet(barrier, at_rank(r)))
    for c in locals_:
        c.wait()
    wp[0] = jnp.zeros((8, n), F32)
    wp[0, 0:1, :] = w_in[...]
    wp[0, 1:2, :] = p_in[...].astype(F32)
    pl.semaphore_wait(barrier, 4 + rank)

    def u_rows(slot, h):
        return u_all.at[pl.ds(slot * n + h * half, half)]

    def i_rows(slot, h):
        return i_all.at[pl.ds(slot * n + h * half, half)]

    started = []

    def start(copy):
        copy.start()
        started.append(copy)
        return copy

    wp_r = start(remote(wp.at[0], wp.at[1], WP_RIGHT, right))
    wp_l = start(remote(wp.at[0], wp.at[3], WP_LEFT, left))
    u_r0 = start(remote(u_rows(0, 0), u_rows(1, 0), U_RIGHT_0, right))
    u_l1 = start(remote(u_rows(0, 1), u_rows(3, 1), U_LEFT_1, left))
    i_y0 = start(remote(i_rows(0, 0), i_rows(2, 0), I_Y_0, at_yc(2)))
    i_core = start(remote(i_all.at[pl.ds(0, n)], i_all.at[pl.ds(n, n)], I_CORE, at_yc(1)))
    u_r1 = start(remote(u_rows(0, 1), u_rows(1, 1), U_RIGHT_1, right))
    u_l0 = start(remote(u_rows(0, 0), u_rows(3, 0), U_LEFT_0, left))
    i_y1 = start(remote(i_rows(0, 1), i_rows(2, 1), I_Y_1, at_yc(2)))
    loop(0, rank, lambda r: greet(hello, at_rank(r)))

    k = jnp.exp(jnp.full((1, 2 * n), log_scale[0], F32)) * (1.0 / (math.sqrt(width) * math.log(2.0)))

    def scores(slot, h):
        block = dot_nt(u_all[slot * n : (slot + 1) * n, :], i_all[h * 2 * n : (h + 1) * 2 * n, :])
        t_all[slot * n : (slot + 1) * n, h * 2 * n : (h + 1) * 2 * n] = block * k

    lane = lax.broadcasted_iota(jnp.int32, (1, 128), 1)

    def column_ids(c):
        block, part = c // per, c % per
        owner = at_yc(block)["blk"]
        return (owner * n + part * 128 + lane).astype(F32)

    ids = [column_ids(c) for c in range(chunks)]

    def spread(slot):
        wcol[slot * n : (slot + 1) * n, :] = jnp.broadcast_to(wp[slot, 0:1, :], (128, n)).T
        pcol[slot * n : (slot + 1) * n, :] = jnp.broadcast_to(wp[slot, 1:2, :], (128, n)).T

    def statistics(slot):
        def maxima(i, best):
            rows = pl.ds(pl.multiple_of(slot * n + i * CHUNK, CHUNK), CHUNK)
            top = None
            out = []
            for c in range(chunks):
                t = t_all[rows, c * 128 : (c + 1) * 128]
                top = t if top is None else jnp.maximum(top, t)
                out.append(jnp.maximum(best[c], fold_rows(t, jnp.maximum)))
            here = pl.ds(pl.multiple_of(i * CHUNK, CHUNK), CHUNK)
            row_m[here, :] = jnp.broadcast_to(jnp.max(top, axis=1, keepdims=True), (CHUNK, 128))
            return tuple(out)

        best = lax.fori_loop(
            0, steps, maxima, tuple(jnp.full((8, 128), LOW, F32) for _ in range(chunks)), unroll=True
        )
        best = [jnp.max(b, axis=0, keepdims=True) for b in best]

        def sums(i, total):
            rows = pl.ds(pl.multiple_of(slot * n + i * CHUNK, CHUNK), CHUNK)
            here = pl.ds(pl.multiple_of(i * CHUNK, CHUNK), CHUNK)
            m = row_m[here, :]
            p = pcol[rows, :]
            w = wcol[rows, :]
            out = []
            line = None
            for c in range(chunks):
                t = t_all[rows, c * 128 : (c + 1) * 128]
                d = t - m
                e = jnp.exp2(d)
                cd = t - best[c]
                ce = jnp.exp2(cd)
                at = p == ids[c]
                hit = jnp.where(at, t, 0.0)
                new = (e, e * d, hit)
                line = new if line is None else tuple(a + b for a, b in zip(line, new))
                for q, v in enumerate((ce, ce * cd, hit, jnp.where(at, w, 0.0))):
                    out.append(total[4 * c + q] + fold_rows(v, jnp.add))
            for q in range(3):
                lines[q, here, :] = line[q]
            return tuple(out)

        total = lax.fori_loop(
            0, steps, sums, tuple(jnp.zeros((8, 128), F32) for _ in range(4 * chunks)), unroll=True
        )
        total = [jnp.sum(b, axis=0, keepdims=True) for b in total]
        rowst[0, slot : slot + 1, :] = row_m[...].T[0:1, :]
        for q in range(3):
            at = (q + 1) * nx + slot
            rowst[0, at : at + 1, :] = jnp.sum(lines[q].T, axis=0, keepdims=True)
        return best, total

    parts = {}
    spread(0)
    i_core.wait_recv()
    scores(0, 0)
    wp_r.wait_recv()
    wp_relay = start(remote(wp.at[1], wp.at[2], WP_RELAY, right))
    spread(1)
    wp_l.wait_recv()
    spread(3)
    u_r0.wait_recv()
    relay_r = start(remote(u_rows(1, 0), u_rows(2, 0), U_RELAY_RIGHT, right))
    u_l1.wait_recv()
    relay_l = start(remote(u_rows(3, 1), u_rows(2, 1), U_RELAY_LEFT, left))
    i_y0.wait_recv()
    i_p0 = start(remote(i_rows(2, 0), i_rows(3, 0), I_PASS_0, at_yc(1)))
    wp_relay.wait_recv()
    spread(2)
    u_r1.wait_recv()
    scores(1, 0)
    u_l0.wait_recv()
    scores(3, 0)
    i_y1.wait_recv()
    i_p1 = start(remote(i_rows(2, 1), i_rows(3, 1), I_PASS_1, at_yc(1)))
    i_p0.wait_recv()
    i_p1.wait_recv()
    for slot in (0, 1, 3):
        scores(slot, 1)
        parts[slot] = statistics(slot)
    relay_r.wait_recv()
    relay_l.wait_recv()
    scores(2, 0)
    scores(2, 1)
    parts[2] = statistics(2)

    rs_copies = [start(remote(rowst.at[0], rowst.at[d], RS_1 + d - 1, at_x(d))) for d in (2, 1, 3)]
    colst[0] = jnp.zeros((24, n), F32)
    for c in range(chunks):
        b, q = c // per, (c % per) * 128
        ms = [parts[s][0][c] for s in range(nx)]
        m = functools.reduce(jnp.maximum, ms)
        l = e = 0.0
        for s in range(nx):
            scale = jnp.exp2(ms[s] - m)
            part_l = parts[s][1][4 * c]
            l = l + scale * part_l
            e = e + scale * (parts[s][1][4 * c + 1] + (ms[s] - m) * part_l)
        hit = sum(parts[s][1][4 * c + 2] for s in range(nx))
        cw = sum(parts[s][1][4 * c + 3] for s in range(nx))
        for i, v in enumerate((m, l, e, hit, cw)):
            colst[0, i * nyc + b : i * nyc + b + 1, q : q + 128] = v
    cs_copies = [start(remote(colst.at[0], colst.at[d], CS_1 + d - 1, at_yc(d))) for d in (3, 2, 1)]

    def combine(source, at, count):
        def rows(i):
            return [source[d, i * count + at[d] : i * count + at[d] + 1, :] for d in range(count)]

        ms, ls, es, hits = rows(0), rows(1), rows(2), rows(3)
        m = functools.reduce(jnp.maximum, ms)
        scales = [jnp.exp2(mi - m) for mi in ms]
        l = sum(li * si for li, si in zip(ls, scales))

        def share():
            e = sum(si * (ei + (mi - m) * li) for mi, li, ei, si in zip(ms, ls, es, scales))
            return e / l - (sum(hits) - m)

        return m, l, share

    for c in cs_copies:
        c.wait_recv()
    part = 0.0
    for b in range(nyc):
        at = [b ^ d for d in range(nyc)]
        m, l, share = combine(colst, at, nyc)
        w = sum(colst[d, 4 * nyc + at[d] : 4 * nyc + at[d] + 1, :] for d in range(nyc))
        brow[0:1, b * n : (b + 1) * n] = m + jnp.log2(l / w)
        if b == 0:
            part = part + w * share()
    for c in rs_copies:
        c.wait_recv()
    for r in (0, 2, 1, 3):
        m, l, share = combine(rowst, [(r - d) % nx for d in range(nx)], nx)
        w = wp[r, 0:1, :]
        if r == 0:
            part = part + w * share()
            red_dp[rank] = jnp.zeros((8, 128), F32)
            red_dp[rank, 0:1, :] = jnp.broadcast_to(
                jnp.sum(part, axis=1, keepdims=True) * math.log(2.0), (1, 128)
            )
            red_dp[rank, 1:2, :] = jnp.broadcast_to(jnp.sum(w, axis=1, keepdims=True), (1, 128))

            def dp_send_to(r):
                return pltpu.make_async_remote_copy(
                    src_ref=red_dp.at[rank], dst_ref=red_dp.at[rank], send_sem=dp_send.at[r],
                    recv_sem=dp_recv.at[rank], device_id=at_rank(r), device_id_type=MESH,
                )

            def dp_from(r):
                return pltpu.make_async_remote_copy(
                    src_ref=red_dp.at[rank], dst_ref=red_dp.at[r], send_sem=dp_send.at[r],
                    recv_sem=dp_recv.at[r], device_id=at_rank(r), device_id_type=MESH,
                )

            loop(0, rank, lambda r: dp_send_to(r).start())
        a = m + jnp.log2(l / w)
        acol[r * n : (r + 1) * n, :] = jnp.broadcast_to(a, (128, n)).T

    b_rows = [brow[0:1, c * 128 : (c + 1) * 128] for c in range(chunks)]

    def gradients(slot):
        def step(i, carry):
            rows = pl.ds(pl.multiple_of(slot * n + i * CHUNK, CHUNK), CHUNK)
            a = acol[rows, :]
            w2 = 2.0 * wcol[rows, :]
            p = pcol[rows, :]
            for c in range(chunks):
                t = t_all[rows, c * 128 : (c + 1) * 128]
                g = jnp.exp2(t - a) + jnp.exp2(t - b_rows[c])
                g = g - jnp.where(p == ids[c], w2, 0.0)
                g_all[rows, c * 128 : (c + 1) * 128] = g.astype(BF16)
            return carry

        lax.fori_loop(0, steps, step, 0, unroll=True)

    def user_part(slot):
        return jnp.dot(
            g_all[slot * n : (slot + 1) * n, :], i_all[...], preferred_element_type=F32
        )

    def item_part(slot):
        return dot_tn(g_all[:, slot * n : (slot + 1) * n], u_all[...])

    gradients(2)
    far[...] = user_part(2).astype(BF16)
    gu_fr = start(remote(far.at[pl.ds(0, half)], far_right, GU_FAR_RIGHT, right))
    gu_fl = start(remote(far.at[pl.ds(half, half)], far_left, GU_FAR_LEFT, left))
    gradients(1)
    own_gu[...] = user_part(1)
    to_left[0:half, :] = own_gu[0:half, :].astype(BF16)
    gu_l0 = start(remote(to_left.at[pl.ds(0, half)], from_right.at[pl.ds(0, half)], GU_LEFT_0, left))
    gradients(3)
    own_gi[...] = user_part(3)
    to_right[half:n, :] = own_gi[half:n, :].astype(BF16)
    gu_r1 = start(
        remote(to_right.at[pl.ds(half, half)], from_left.at[pl.ds(half, half)], GU_RIGHT_1, right)
    )
    gradients(0)
    core_1[...] = item_part(3).astype(BF16)
    gi_c1 = start(remote(core_1, got_core_1, GI_CORE_1, at_yc(1)))
    core_0[...] = item_part(1).astype(BF16)
    gi_c0 = start(remote(core_0, got_core_0, GI_CORE_0, at_yc(1)))
    other_gi[...] = item_part(2)
    gi_c1.wait_recv()
    to_y[...] = (other_gi[...] + got_core_1[...].astype(F32)).astype(BF16)
    gi_y = start(remote(to_y, from_y, GI_Y, at_yc(2)))

    gu_fr.wait_recv()
    to_right[0:half, :] = (own_gi[0:half, :] + far_right[...].astype(F32)).astype(BF16)
    gu_r0 = start(
        remote(to_right.at[pl.ds(0, half)], from_left.at[pl.ds(0, half)], GU_RIGHT_0, right)
    )
    gu_fl.wait_recv()
    to_left[half:n, :] = (own_gu[half:n, :] + far_left[...].astype(F32)).astype(BF16)
    gu_l1 = start(
        remote(to_left.at[pl.ds(half, half)], from_right.at[pl.ds(half, half)], GU_LEFT_1, left)
    )
    own_gu[...] = user_part(0)
    own_gi[...] = item_part(0)
    gi_c0.wait_recv()
    own_gi[...] = own_gi[...] + got_core_0[...].astype(F32)
    gu_l0.wait_recv()
    gu_r1.wait_recv()
    gu_r0.wait_recv()
    gu_l1.wait_recv()
    own_gu[...] = own_gu[...] + from_left[...].astype(F32) + from_right[...].astype(F32)
    gi_y.wait_recv()
    own_gi[...] = own_gi[...] + from_y[...].astype(F32)

    @pl.when(rank < n_dp - 1)
    def _():
        pl.semaphore_wait(hello, n_dp - 1 - rank)

    loop(rank + 1, n_dp, lambda r: dp_send_to(r).start())
    loop(0, rank, lambda r: dp_from(r).wait_recv())
    loop(rank + 1, n_dp, lambda r: dp_from(r).wait_recv())
    red_blk[0] = jnp.sum(red_dp[...], axis=0)

    def blk_copy(d):
        return pltpu.make_async_remote_copy(
            src_ref=red_blk.at[0], dst_ref=red_blk.at[d], send_sem=blk_send.at[d], recv_sem=blk_recv.at[d],
            device_id={"blk": (me + d) % n_blk, "dp": my_dp}, device_id_type=MESH,
        )

    loop(1, n_blk, lambda d: blk_copy(d).start())
    loop(1, n_blk, lambda d: blk_copy(d).wait_recv())
    sums = jnp.sum(red_blk[...], axis=0)
    weight = sums[1:2, :]
    scale_out[0] = (sums[0:1, :] / weight)[0, 0]
    rows_total = float(n * n_blk * n_dp)
    factor = (rows_total / weight) * (k[:, 0:128] * math.log(2.0))
    factor = jnp.concatenate([factor] * (width // 128), axis=1)
    gu_out[...] = (factor * own_gu[...]).astype(BF16)
    gi_out[...] = (factor * own_gi[...]).astype(BF16)

    for c in started:
        c.wait_send()
    loop(0, rank, lambda r: dp_send_to(r).wait_send())
    loop(rank + 1, n_dp, lambda r: dp_send_to(r).wait_send())
    loop(1, n_blk, lambda d: blk_copy(d).wait_send())


def body(users, items, weights, positives, log_scale):
    users, items = users[0], items[0]
    n, width = users.shape
    n_blk, n_dp = lax.axis_size("blk"), lax.axis_size("dp")
    nyc = 4
    nx = n_blk // nyc
    any_space = pl.BlockSpec(memory_space=pl.ANY)
    vmem = pl.BlockSpec(memory_space=pltpu.VMEM)
    smem = pl.BlockSpec(memory_space=pltpu.SMEM)
    V = pltpu.VMEM
    rows, cols = nx * n, nyc * n
    half = n // 2
    gu, gi, scale = pl.pallas_call(
        functools.partial(kernel, nx, nyc, n_dp, n_blk),
        out_shape=(
            jax.ShapeDtypeStruct((n, width), BF16),
            jax.ShapeDtypeStruct((n, width), BF16),
            jax.ShapeDtypeStruct((1,), F32),
        ),
        in_specs=[any_space, any_space, any_space, any_space, smem],
        out_specs=(vmem, vmem, smem),
        scratch_shapes=[
            V((rows, width), BF16),
            V((cols, width), BF16),
            V((1, n), F32),
            V((1, n), jnp.int32),
            V((nx, 8, n), F32),
            V((rows, cols), F32),
            V((rows, cols), BF16),
            V((rows, 128), F32),
            V((rows, 128), F32),
            V((rows, 128), F32),
            V((n, 128), F32),
            V((3, n, 128), F32),
            V((nx, 16, n), F32),
            V((nyc, 24, n), F32),
            V((8, cols), F32),
            V((n, width), BF16),
            V((half, width), BF16),
            V((half, width), BF16),
            V((n, width), BF16),
            V((n, width), BF16),
            V((n, width), BF16),
            V((n, width), BF16),
            V((n, width), F32),
            V((n, width), F32),
            V((n, width), F32),
            V((n, width), BF16),
            V((n, width), BF16),
            V((n, width), BF16),
            V((n, width), BF16),
            V((n, width), BF16),
            V((n, width), BF16),
            V((n_dp, 8, 128), F32),
            V((n_blk, 8, 128), F32),
            pltpu.SemaphoreType.DMA((4,)),
            pltpu.SemaphoreType.DMA((TRANSFERS,)),
            pltpu.SemaphoreType.DMA((TRANSFERS,)),
            pltpu.SemaphoreType.DMA((n_dp,)),
            pltpu.SemaphoreType.DMA((n_dp,)),
            pltpu.SemaphoreType.DMA((n_blk,)),
            pltpu.SemaphoreType.DMA((n_blk,)),
            pltpu.SemaphoreType.REGULAR,
        ],
        compiler_params=pltpu.CompilerParams(
            collective_id=0, has_side_effects=True, vmem_limit_bytes=60 * 1024 * 1024
        ),
        cost_estimate=pl.CostEstimate(
            flops=6 * rows * cols * width, bytes_accessed=4 * n * width * 2,
            transcendentals=4 * rows * cols,
        ),
        name="loss_gradients",
    )(users, items, weights, positives, log_scale)
    return gu[None], gi[None], scale


def solution(mesh):
    placed = (P("dp", "blk", None), P("dp", "blk", None), P("dp", "blk"), P("dp", "blk"), P())
    return jax.shard_map(
        body,
        mesh=mesh,
        in_specs=placed,
        out_specs=(P("dp", "blk", None), P("dp", "blk", None), P()),
        check_vma=False,
    )
```

time: 67.8 us -> 58.6 us (0.86)
  the two profiles are of different devices: /device:TPU:1 before, /device:TPU:481 now
where the time goes in v2:
time: 58.6 us; the launch traced here: 58.4 us
  Pallas kernels  53 us (90%)
  between operations  3.06 us (5%)
  local copies, waits for them, and re-layouts  2.42 us (4%)
    pallas_call x1, Pallas kernels, body(): pl.pallas_call(functools.partial(kernel, nx, nyc, n_dp, n_blk), out_shape...  53 us
    unnamed x4, local copies, waits for them, and re-layouts  2.42 us

profile of v2, /device:TPU:481, one launch (start us, length us, event | category | flops | bytes accessed | tf_op | source)
XLA Modules:
  0.0 58.4 jit_solution(2621239169117570942)
XLA Ops:
  1.3 53.0 %loss_gradients.1 = (bf16[256,512]{1,0:T(8,128)(2,1)}, bf16[256,512]{1,0:T(8,128)(2,1)}, f32[1]{0:T(128)}) custom-call(bf16[256,512]{1,0:T(8,128)(2,1)} %bitcast.6, bf16[256,512]{1,0:T(8,128)(2,1)} %bitcast.7, f32[1,256]{1,0:T(1,128)} %weights.1, s32[1,256]{1,0:T(1,128)} %positives.1, f32[1]{0:T(128)S(6)} %copy.11.log_scale), custom_call_target="tpu_custom_call" | custom-call | flops 3221225472 | bytes 1048576 | tf_op jit(solution)/shard_map/loss_gradients/pallas_call | solution.py:439
  54.2 0.0 copy-start
  54.2 1.7 %copy.12 = bf16[1,256,512]{2,1,0:T(8,128)(2,1)} copy(bf16[1,256,512]{2,1,0:T(8,128)(2,1)} %bitcast.5) | data formatting | bytes 524288
  56.0 0.0 copy-done
  56.0 0.7 %copy.13 = bf16[1,256,512]{2,1,0:T(8,128)(2,1)} copy(bf16[1,256,512]{2,1,0:T(8,128)(2,1)S(1)} %bitcast.4) | data formatting | bytes 524288
Async XLA Ops:
  54.2 1.7 %copy-start = (bf16[256,512]{1,0:T(8,128)(2,1)S(1)}, bf16[256,512]{1,0:T(8,128)(2,1)}, u32[]{:S(2)}) copy-start(bf16[256,512]{1,0:T(8,128)(2,1)} %get-tuple-element.7) | copy-start | bytes 786436

commit v3 on v2

--- a/solution.py
+++ b/solution.py
@@ -47,8 +47,8 @@
     rowst, colst, brow,
     far, far_right, far_left, to_left, to_right, from_left, from_right,
     own_gu, own_gi, other_gi, core_0, core_1, got_core_0, got_core_1, to_y, from_y,
-    red_dp, red_blk,
-    local_sem, send, recv, dp_send, dp_recv, blk_send, blk_recv, hello,
+    red_z, red_plane, totals,
+    local_sem, send, recv, z_send, z_recv, plane_send, plane_recv, all_send, all_recv, ready,
 ):
     n = users.shape[0]
     width = users.shape[1]
@@ -64,7 +64,8 @@
     core = yc % 2
     y = yc // 2
     depth = n_dp // 2
-    rank = (my_dp % depth) * 2 + my_dp // depth
+    z = my_dp % depth
+    high = my_dp // depth
 
     def at_x(d):
         return {"blk": ((x + d) % nx) * nyc + yc, "dp": my_dp}
@@ -74,8 +75,13 @@
         w = 1 - y if d // 2 else y
         return {"blk": x * nyc + w * 2 + c, "dp": my_dp}
 
-    def at_rank(r):
-        return {"blk": me, "dp": (r % 2) * depth + r // 2}
+    def at_z(to):
+        return {"blk": me, "dp": high * depth + to}
+
+    def at_plane(p):
+        return {"blk": p % n_blk, "dp": (p // n_blk) * depth}
+
+    other_group = {"blk": me, "dp": (1 - high) * depth + z}
 
     right, left = at_x(1), at_x(nx - 1)
 
@@ -102,22 +108,26 @@
         pltpu.make_async_copy(src, dst, local_sem.at[i])
         for i, (src, dst) in enumerate(
             [
+                (weights, w_in),
+                (positives, p_in),
                 (users, u_all.at[pl.ds(0, n)]),
                 (items, i_all.at[pl.ds(0, n)]),
-                (weights, w_in),
-                (positives, p_in),
             ]
         )
     ]
     for c in locals_:
         c.start()
-    loop(rank + 1, n_dp, lambda r: greet(barrier, at_rank(r)))
-    for c in locals_:
-        c.wait()
+
+    @pl.when(z == 0)
+    def _():
+        loop(1, depth, lambda to: greet(barrier, at_z(to)))
+
+        @pl.when(high == 0)
+        def _():
+            greet(barrier, other_group)
+
     wp[0] = jnp.zeros((8, n), F32)
-    wp[0, 0:1, :] = w_in[...]
-    wp[0, 1:2, :] = p_in[...].astype(F32)
-    pl.semaphore_wait(barrier, 4 + rank)
+    pl.semaphore_wait(barrier, 4 + jnp.where(my_dp == 0, 0, 1))
 
     def u_rows(slot, h):
         return u_all.at[pl.ds(slot * n + h * half, half)]
@@ -132,16 +142,24 @@
         started.append(copy)
         return copy
 
+    def piece(ref, h):
+        return ref.at[pl.ds(h * half, half)]
+
+    u_r0 = start(remote(piece(users, 0), u_rows(1, 0), U_RIGHT_0, right))
+    u_l1 = start(remote(piece(users, 1), u_rows(3, 1), U_LEFT_1, left))
+    i_y0 = start(remote(piece(items, 0), i_rows(2, 0), I_Y_0, at_yc(2)))
+    i_core = start(remote(items, i_all.at[pl.ds(n, n)], I_CORE, at_yc(1)))
+    locals_[0].wait()
+    locals_[1].wait()
+    wp[0, 0:1, :] = w_in[...]
+    wp[0, 1:2, :] = p_in[...].astype(F32)
     wp_r = start(remote(wp.at[0], wp.at[1], WP_RIGHT, right))
     wp_l = start(remote(wp.at[0], wp.at[3], WP_LEFT, left))
-    u_r0 = start(remote(u_rows(0, 0), u_rows(1, 0), U_RIGHT_0, right))
-    u_l1 = start(remote(u_rows(0, 1), u_rows(3, 1), U_LEFT_1, left))
-    i_y0 = start(remote(i_rows(0, 0), i_rows(2, 0), I_Y_0, at_yc(2)))
-    i_core = start(remote(i_all.at[pl.ds(0, n)], i_all.at[pl.ds(n, n)], I_CORE, at_yc(1)))
-    u_r1 = start(remote(u_rows(0, 1), u_rows(1, 1), U_RIGHT_1, right))
-    u_l0 = start(remote(u_rows(0, 0), u_rows(3, 0), U_LEFT_0, left))
-    i_y1 = start(remote(i_rows(0, 1), i_rows(2, 1), I_Y_1, at_yc(2)))
-    loop(0, rank, lambda r: greet(hello, at_rank(r)))
+    u_r1 = start(remote(piece(users, 1), u_rows(1, 1), U_RIGHT_1, right))
+    u_l0 = start(remote(piece(users, 0), u_rows(3, 0), U_LEFT_0, left))
+    i_y1 = start(remote(piece(items, 1), i_rows(2, 1), I_Y_1, at_yc(2)))
+    locals_[2].wait()
+    locals_[3].wait()
 
     k = jnp.exp(jnp.full((1, 2 * n), log_scale[0], F32)) * (1.0 / (math.sqrt(width) * math.log(2.0)))
 
@@ -281,44 +299,47 @@
 
         return m, l, share
 
+    def column_stats(b):
+        at = [b ^ d for d in range(nyc)]
+        w = sum(colst[d, 4 * nyc + at[d] : 4 * nyc + at[d] + 1, :] for d in range(nyc))
+        return combine(colst, at, nyc) + (w,)
+
+    def row_stats(r):
+        return combine(rowst, [(r - d) % nx for d in range(nx)], nx) + (wp[r, 0:1, :],)
+
     for c in cs_copies:
         c.wait_recv()
-    part = 0.0
-    for b in range(nyc):
-        at = [b ^ d for d in range(nyc)]
-        m, l, share = combine(colst, at, nyc)
-        w = sum(colst[d, 4 * nyc + at[d] : 4 * nyc + at[d] + 1, :] for d in range(nyc))
-        brow[0:1, b * n : (b + 1) * n] = m + jnp.log2(l / w)
-        if b == 0:
-            part = part + w * share()
+    column_0 = column_stats(0)
+    part = column_0[3] * column_0[2]()
     for c in rs_copies:
         c.wait_recv()
-    for r in (0, 2, 1, 3):
-        m, l, share = combine(rowst, [(r - d) % nx for d in range(nx)], nx)
-        w = wp[r, 0:1, :]
-        if r == 0:
-            part = part + w * share()
-            red_dp[rank] = jnp.zeros((8, 128), F32)
-            red_dp[rank, 0:1, :] = jnp.broadcast_to(
-                jnp.sum(part, axis=1, keepdims=True) * math.log(2.0), (1, 128)
-            )
-            red_dp[rank, 1:2, :] = jnp.broadcast_to(jnp.sum(w, axis=1, keepdims=True), (1, 128))
-
-            def dp_send_to(r):
-                return pltpu.make_async_remote_copy(
-                    src_ref=red_dp.at[rank], dst_ref=red_dp.at[rank], send_sem=dp_send.at[r],
-                    recv_sem=dp_recv.at[rank], device_id=at_rank(r), device_id_type=MESH,
-                )
-
-            def dp_from(r):
-                return pltpu.make_async_remote_copy(
-                    src_ref=red_dp.at[rank], dst_ref=red_dp.at[r], send_sem=dp_send.at[r],
-                    recv_sem=dp_recv.at[r], device_id=at_rank(r), device_id_type=MESH,
-                )
-
-            loop(0, rank, lambda r: dp_send_to(r).start())
-        a = m + jnp.log2(l / w)
-        acol[r * n : (r + 1) * n, :] = jnp.broadcast_to(a, (128, n)).T
+    row_0 = row_stats(0)
+    part = part + row_0[3] * row_0[2]()
+
+    red_z[z] = jnp.zeros((8, 128), F32)
+    red_z[z, 0:1, :] = jnp.broadcast_to(jnp.sum(part, axis=1, keepdims=True) * math.log(2.0), (1, 128))
+    red_z[z, 1:2, :] = jnp.broadcast_to(jnp.sum(row_0[3], axis=1, keepdims=True), (1, 128))
+
+    def z_copy(source, to):
+        return pltpu.make_async_remote_copy(
+            src_ref=red_z.at[source], dst_ref=red_z.at[source], send_sem=z_send.at[0],
+            recv_sem=z_recv.at[source], device_id=at_z(to), device_id_type=MESH,
+        )
+
+    @pl.when(z > 0)
+    def _():
+        z_copy(z, 0).start()
+
+    @pl.when((z == 0) & (high == 1))
+    def _():
+        greet(ready, other_group)
+
+    for b in range(nyc):
+        m, l, _, w = column_stats(b) if b else column_0
+        brow[0:1, b * n : (b + 1) * n] = m + jnp.log2(l / w)
+    for r in (2, 1, 3, 0):
+        m, l, _, w = row_stats(r) if r else row_0
+        acol[r * n : (r + 1) * n, :] = jnp.broadcast_to(m + jnp.log2(l / w), (128, n)).T
 
     b_rows = [brow[0:1, c * 128 : (c + 1) * 128] for c in range(chunks)]
 
@@ -391,24 +412,45 @@
     gi_y.wait_recv()
     own_gi[...] = own_gi[...] + from_y[...].astype(F32)
 
-    @pl.when(rank < n_dp - 1)
+    def plane_copy(source, to):
+        return pltpu.make_async_remote_copy(
+            src_ref=red_plane.at[source], dst_ref=red_plane.at[source], send_sem=plane_send.at[to],
+            recv_sem=plane_recv.at[source], device_id=at_plane(to), device_id_type=MESH,
+        )
+
+    def all_copy(to):
+        return pltpu.make_async_remote_copy(
+            src_ref=totals, dst_ref=totals, send_sem=all_send.at[to], recv_sem=all_recv.at[0],
+            device_id=at_z(to), device_id_type=MESH,
+        )
+
+    @pl.when(z == 0)
     def _():
-        pl.semaphore_wait(hello, n_dp - 1 - rank)
-
-    loop(rank + 1, n_dp, lambda r: dp_send_to(r).start())
-    loop(0, rank, lambda r: dp_from(r).wait_recv())
-    loop(rank + 1, n_dp, lambda r: dp_from(r).wait_recv())
-    red_blk[0] = jnp.sum(red_dp[...], axis=0)
-
-    def blk_copy(d):
-        return pltpu.make_async_remote_copy(
-            src_ref=red_blk.at[0], dst_ref=red_blk.at[d], send_sem=blk_send.at[d], recv_sem=blk_recv.at[d],
-            device_id={"blk": (me + d) % n_blk, "dp": my_dp}, device_id_type=MESH,
-        )
-
-    loop(1, n_blk, lambda d: blk_copy(d).start())
-    loop(1, n_blk, lambda d: blk_copy(d).wait_recv())
-    sums = jnp.sum(red_blk[...], axis=0)
+        here = high * n_blk + me
+        pl.semaphore_wait(ready, 1)
+
+        @pl.when(high == 0)
+        def _():
+            greet(ready, other_group)
+
+        loop(1, depth, lambda source: z_copy(source, 0).wait_recv())
+        red_plane[here] = jnp.sum(red_z[...], axis=0)
+        loop(0, here, lambda to: plane_copy(here, to).start())
+        loop(here + 1, 2 * n_blk, lambda to: plane_copy(here, to).start())
+        loop(0, here, lambda source: plane_copy(source, source).wait_recv())
+        loop(here + 1, 2 * n_blk, lambda source: plane_copy(source, source).wait_recv())
+        totals[...] = jnp.sum(red_plane[...], axis=0)
+        loop(1, depth, lambda to: all_copy(to).start())
+        loop(0, here, lambda to: plane_copy(here, to).wait_send())
+        loop(here + 1, 2 * n_blk, lambda to: plane_copy(here, to).wait_send())
+        loop(1, depth, lambda to: all_copy(to).wait_send())
+
+    @pl.when(z > 0)
+    def _():
+        all_copy(0).wait_recv()
+        z_copy(z, 0).wait_send()
+
+    sums = totals[...]
     weight = sums[1:2, :]
     scale_out[0] = (sums[0:1, :] / weight)[0, 0]
     rows_total = float(n * n_blk * n_dp)
@@ -419,9 +461,6 @@
 
     for c in started:
         c.wait_send()
-    loop(0, rank, lambda r: dp_send_to(r).wait_send())
-    loop(rank + 1, n_dp, lambda r: dp_send_to(r).wait_send())
-    loop(1, n_blk, lambda d: blk_copy(d).wait_send())
 
 
 def body(users, items, weights, positives, log_scale):
@@ -439,8 +478,8 @@
     gu, gi, scale = pl.pallas_call(
         functools.partial(kernel, nx, nyc, n_dp, n_blk),
         out_shape=(
-            jax.ShapeDtypeStruct((n, width), BF16),
-            jax.ShapeDtypeStruct((n, width), BF16),
+            pltpu.VMEM((n, width), BF16),
+            pltpu.VMEM((n, width), BF16),
             jax.ShapeDtypeStruct((1,), F32),
         ),
         in_specs=[any_space, any_space, any_space, any_space, smem],
@@ -477,15 +516,18 @@
             V((n, width), BF16),
             V((n, width), BF16),
             V((n, width), BF16),
-            V((n_dp, 8, 128), F32),
-            V((n_blk, 8, 128), F32),
+            V((n_dp // 2, 8, 128), F32),
+            V((2 * n_blk, 8, 128), F32),
+            V((8, 128), F32),
             pltpu.SemaphoreType.DMA((4,)),
             pltpu.SemaphoreType.DMA((TRANSFERS,)),
             pltpu.SemaphoreType.DMA((TRANSFERS,)),
-            pltpu.SemaphoreType.DMA((n_dp,)),
-            pltpu.SemaphoreType.DMA((n_dp,)),
-            pltpu.SemaphoreType.DMA((n_blk,)),
-            pltpu.SemaphoreType.DMA((n_blk,)),
+            pltpu.SemaphoreType.DMA((1,)),
+            pltpu.SemaphoreType.DMA((n_dp // 2,)),
+            pltpu.SemaphoreType.DMA((2 * n_blk,)),
+            pltpu.SemaphoreType.DMA((2 * n_blk,)),
+            pltpu.SemaphoreType.DMA((n_dp // 2,)),
+            pltpu.SemaphoreType.DMA((1,)),
             pltpu.SemaphoreType.REGULAR,
         ],
         compiler_params=pltpu.CompilerParams(

time: 58.6 us -> 51 us (0.87)
  the two profiles are of different devices: /device:TPU:481 before, /device:TPU:1 now
where the time goes in v3:
time: 51 us; the launch traced here: 50.9 us
  Pallas kernels  46.5 us (91%)
  between operations  2.98 us (6%)
  local copies, waits for them, and re-layouts  1.41 us (3%)
    pallas_call x1, Pallas kernels, body(): pl.pallas_call(functools.partial(kernel, nx, nyc, n_dp, n_blk), out_shape...  46.5 us
    unnamed x2, local copies, waits for them, and re-layouts  1.41 us

profile of v3, /device:TPU:1, one launch (start us, length us, event | category | flops | bytes accessed | tf_op | source)
XLA Modules:
  0.0 50.9 jit_solution(2768258046625722134)
XLA Ops:
  1.3 46.5 %loss_gradients.1 = (bf16[256,512]{1,0:T(8,128)(2,1)S(1)}, bf16[256,512]{1,0:T(8,128)(2,1)S(1)}, f32[1]{0:T(128)}) custom-call(bf16[256,512]{1,0:T(8,128)(2,1)} %bitcast.6, bf16[256,512]{1,0:T(8,128)(2,1)} %bitcast.7, f32[1,256]{1,0:T(1,128)} %weights.1, s32[1,256]{1,0:T(1,128)} %positives.1, f32[1]{0:T(128)S(6)} %copy.13.log_scale), custom_call_target="tpu_custom_call" | custom-call | flops 3221225472 | bytes 1048576 | tf_op jit(solution)/shard_map/loss_gradients/pallas_call | solution.py:478
  47.8 0.7 %copy.11 = bf16[1,256,512]{2,1,0:T(8,128)(2,1)} copy(bf16[1,256,512]{2,1,0:T(8,128)(2,1)S(1)} %bitcast.5) | data formatting | bytes 524288
  48.5 0.7 %copy.12 = bf16[1,256,512]{2,1,0:T(8,128)(2,1)} copy(bf16[1,256,512]{2,1,0:T(8,128)(2,1)S(1)} %bitcast.4) | data formatting | bytes 524288

commit v4 on v3

--- a/solution.py
+++ b/solution.py
@@ -16,12 +16,12 @@
 
 (
     U_RIGHT_0, U_LEFT_1, U_RIGHT_1, U_LEFT_0, U_RELAY_RIGHT, U_RELAY_LEFT,
-    I_CORE, I_Y_0, I_Y_1, I_PASS_0, I_PASS_1,
-    WP_RIGHT, WP_LEFT, WP_RELAY, RS_1, RS_2, RS_3, CS_1, CS_2, CS_3,
+    I_CORE, I_Y, I_Y_1, I_Y_2, I_Y_3, I_PASS, I_PASS_1, I_PASS_2, I_PASS_3,
+    WP_RIGHT, WP_LEFT, WP_RELAY, RS_1, RS_2, RS_3, CS_1, CS_2, CS_3, RO_1, RO_2, RO_3, CO_1, CO_2, CO_3,
     GU_FAR_RIGHT, GU_FAR_LEFT, GU_RIGHT_0, GU_RIGHT_1, GU_LEFT_0, GU_LEFT_1,
     GI_CORE_0, GI_CORE_1, GI_Y,
     TRANSFERS,
-) = range(30)
+) = range(40)
 
 
 def dot_nt(a, b):
@@ -42,9 +42,9 @@
 def kernel(
     nx, nyc, n_dp, n_blk,
     users, items, weights, positives, log_scale,
-    gu_out, gi_out, scale_out,
+    gu_out, gi_out, scale_out, factor_out,
     u_all, i_all, w_in, p_in, wp, t_all, g_all, wcol, pcol, acol, row_m, lines,
-    rowst, colst, brow,
+    rowst, colst, row_own, col_own, log_in,
     far, far_right, far_left, to_left, to_right, from_left, from_right,
     own_gu, own_gi, other_gi, core_0, core_1, got_core_0, got_core_1, to_y, from_y,
     red_z, red_plane, totals,
@@ -112,6 +112,7 @@
                 (positives, p_in),
                 (users, u_all.at[pl.ds(0, n)]),
                 (items, i_all.at[pl.ds(0, n)]),
+                (log_scale, log_in),
             ]
         )
     ]
@@ -127,13 +128,16 @@
             greet(barrier, other_group)
 
     wp[0] = jnp.zeros((8, n), F32)
+    col_own[0:nyc] = jnp.zeros((nyc, 16, 128), F32)
     pl.semaphore_wait(barrier, 4 + jnp.where(my_dp == 0, 0, 1))
 
     def u_rows(slot, h):
         return u_all.at[pl.ds(slot * n + h * half, half)]
 
-    def i_rows(slot, h):
-        return i_all.at[pl.ds(slot * n + h * half, half)]
+    quarter = n // 4
+
+    def i_rows(slot, q):
+        return i_all.at[pl.ds(slot * n + q * quarter, quarter)]
 
     started = []
 
@@ -147,7 +151,10 @@
 
     u_r0 = start(remote(piece(users, 0), u_rows(1, 0), U_RIGHT_0, right))
     u_l1 = start(remote(piece(users, 1), u_rows(3, 1), U_LEFT_1, left))
-    i_y0 = start(remote(piece(items, 0), i_rows(2, 0), I_Y_0, at_yc(2)))
+    i_y = [
+        start(remote(items.at[pl.ds(q * quarter, quarter)], i_rows(2, q), I_Y + q, at_yc(2)))
+        for q in range(4)
+    ]
     i_core = start(remote(items, i_all.at[pl.ds(n, n)], I_CORE, at_yc(1)))
     locals_[0].wait()
     locals_[1].wait()
@@ -157,15 +164,17 @@
     wp_l = start(remote(wp.at[0], wp.at[3], WP_LEFT, left))
     u_r1 = start(remote(piece(users, 1), u_rows(1, 1), U_RIGHT_1, right))
     u_l0 = start(remote(piece(users, 0), u_rows(3, 0), U_LEFT_0, left))
-    i_y1 = start(remote(piece(items, 1), i_rows(2, 1), I_Y_1, at_yc(2)))
-    locals_[2].wait()
-    locals_[3].wait()
-
-    k = jnp.exp(jnp.full((1, 2 * n), log_scale[0], F32)) * (1.0 / (math.sqrt(width) * math.log(2.0)))
-
-    def scores(slot, h):
-        block = dot_nt(u_all[slot * n : (slot + 1) * n, :], i_all[h * 2 * n : (h + 1) * 2 * n, :])
-        t_all[slot * n : (slot + 1) * n, h * 2 * n : (h + 1) * 2 * n] = block * k
+    for c in locals_[2:]:
+        c.wait()
+
+    k = jnp.exp(jnp.full((1, 2 * n), log_in[0], F32)) * (1.0 / (math.sqrt(width) * math.log(2.0)))
+
+    def scores(slot, first, last):
+        block = dot_nt(u_all[slot * n : (slot + 1) * n, :], i_all[first * n : last * n, :])
+        for b in range(last - first):
+            t_all[slot * n : (slot + 1) * n, (first + b) * n : (first + b + 1) * n] = (
+                block[:, b * n : (b + 1) * n] * k[:, 0:n]
+            )
 
     lane = lax.broadcasted_iota(jnp.int32, (1, 128), 1)
 
@@ -226,50 +235,60 @@
             0, steps, sums, tuple(jnp.zeros((8, 128), F32) for _ in range(4 * chunks)), unroll=True
         )
         total = [jnp.sum(b, axis=0, keepdims=True) for b in total]
-        rowst[0, slot : slot + 1, :] = row_m[...].T[0:1, :]
-        for q in range(3):
-            at = (q + 1) * nx + slot
-            rowst[0, at : at + 1, :] = jnp.sum(lines[q].T, axis=0, keepdims=True)
+        row = [row_m[...].T[0:1, :]] + [jnp.sum(lines[q].T, axis=0, keepdims=True) for q in range(3)]
+        for q in range(4):
+            for h in range(per):
+                v = row[q][:, h * 128 : (h + 1) * 128]
+                row_own[nx - slot, q * per + h : q * per + h + 1, :] = v
+                if q < 2:
+                    at = (q * nx + slot) * per + h
+                    rowst[0, at : at + 1, :] = v
         return best, total
 
     parts = {}
     spread(0)
     i_core.wait_recv()
-    scores(0, 0)
+    scores(0, 0, 2)
     wp_r.wait_recv()
     wp_relay = start(remote(wp.at[1], wp.at[2], WP_RELAY, right))
     spread(1)
     wp_l.wait_recv()
     spread(3)
+
+    i_pass = []
+
+    def pass_on(q):
+        i_y[q].wait_recv()
+        i_pass.append(start(remote(i_rows(2, q), i_rows(3, q), I_PASS + q, at_yc(1))))
+
+    pass_on(0)
     u_r0.wait_recv()
     relay_r = start(remote(u_rows(1, 0), u_rows(2, 0), U_RELAY_RIGHT, right))
     u_l1.wait_recv()
     relay_l = start(remote(u_rows(3, 1), u_rows(2, 1), U_RELAY_LEFT, left))
-    i_y0.wait_recv()
-    i_p0 = start(remote(i_rows(2, 0), i_rows(3, 0), I_PASS_0, at_yc(1)))
+    pass_on(1)
     wp_relay.wait_recv()
     spread(2)
+    pass_on(2)
+    pass_on(3)
+    scores(0, 2, 3)
     u_r1.wait_recv()
-    scores(1, 0)
+    scores(1, 0, 3)
     u_l0.wait_recv()
-    scores(3, 0)
-    i_y1.wait_recv()
-    i_p1 = start(remote(i_rows(2, 1), i_rows(3, 1), I_PASS_1, at_yc(1)))
-    i_p0.wait_recv()
-    i_p1.wait_recv()
+    scores(3, 0, 3)
+    for c in i_pass:
+        c.wait_recv()
     for slot in (0, 1, 3):
-        scores(slot, 1)
+        scores(slot, 3, 4)
         parts[slot] = statistics(slot)
     relay_r.wait_recv()
     relay_l.wait_recv()
-    scores(2, 0)
-    scores(2, 1)
+    scores(2, 0, 4)
     parts[2] = statistics(2)
 
-    rs_copies = [start(remote(rowst.at[0], rowst.at[d], RS_1 + d - 1, at_x(d))) for d in (2, 1, 3)]
-    colst[0] = jnp.zeros((24, n), F32)
+    ro_copies = [start(remote(row_own.at[d], row_own.at[nx + d], RO_1 + d - 1, at_x(d))) for d in (2, 1, 3)]
     for c in range(chunks):
-        b, q = c // per, (c % per) * 128
+        b, h = c // per, c % per
         ms = [parts[s][0][c] for s in range(nx)]
         m = functools.reduce(jnp.maximum, ms)
         l = e = 0.0
@@ -280,45 +299,42 @@
             e = e + scale * (parts[s][1][4 * c + 1] + (ms[s] - m) * part_l)
         hit = sum(parts[s][1][4 * c + 2] for s in range(nx))
         cw = sum(parts[s][1][4 * c + 3] for s in range(nx))
-        for i, v in enumerate((m, l, e, hit, cw)):
-            colst[0, i * nyc + b : i * nyc + b + 1, q : q + 128] = v
+        for q, v in enumerate((m, l, e, hit, cw)):
+            col_own[b, q * per + h : q * per + h + 1, :] = v
+        for q, v in enumerate((m, l, cw)):
+            at = (q * nyc + b) * per + h
+            colst[0, at : at + 1, :] = v
+    co_copies = [start(remote(col_own.at[d], col_own.at[nyc + d], CO_1 + d - 1, at_yc(d))) for d in (3, 2, 1)]
+    rs_copies = [start(remote(rowst.at[0], rowst.at[d], RS_1 + d - 1, at_x(d))) for d in (2, 1, 3)]
     cs_copies = [start(remote(colst.at[0], colst.at[d], CS_1 + d - 1, at_yc(d))) for d in (3, 2, 1)]
 
-    def combine(source, at, count):
-        def rows(i):
-            return [source[d, i * count + at[d] : i * count + at[d] + 1, :] for d in range(count)]
-
-        ms, ls, es, hits = rows(0), rows(1), rows(2), rows(3)
+    def total_share(sources, w):
+        ms, ls, es, hits = ([src(q) for src in sources] for q in range(4))
         m = functools.reduce(jnp.maximum, ms)
         scales = [jnp.exp2(mi - m) for mi in ms]
         l = sum(li * si for li, si in zip(ls, scales))
-
-        def share():
-            e = sum(si * (ei + (mi - m) * li) for mi, li, ei, si in zip(ms, ls, es, scales))
-            return e / l - (sum(hits) - m)
-
-        return m, l, share
-
-    def column_stats(b):
-        at = [b ^ d for d in range(nyc)]
-        w = sum(colst[d, 4 * nyc + at[d] : 4 * nyc + at[d] + 1, :] for d in range(nyc))
-        return combine(colst, at, nyc) + (w,)
-
-    def row_stats(r):
-        return combine(rowst, [(r - d) % nx for d in range(nx)], nx) + (wp[r, 0:1, :],)
-
-    for c in cs_copies:
+        e = sum(si * (ei + (mi - m) * li) for mi, li, ei, si in zip(ms, ls, es, scales))
+        return w * (e / l - (sum(hits) - m))
+
+    def own_rows(ref, i):
+        return lambda q: ref[i, q * per : (q + 1) * per, :]
+
+    for c in co_copies:
         c.wait_recv()
-    column_0 = column_stats(0)
-    part = column_0[3] * column_0[2]()
-    for c in rs_copies:
+    columns = [own_rows(col_own, i) for i in [0] + [nyc + d for d in range(1, nyc)]]
+    part = total_share(columns, sum(src(4) for src in columns))
+    for c in ro_copies:
         c.wait_recv()
-    row_0 = row_stats(0)
-    part = part + row_0[3] * row_0[2]()
+    w_own = jnp.concatenate([wp[0, 0:1, h * 128 : (h + 1) * 128] for h in range(per)], axis=0)
+    part = part + total_share([own_rows(row_own, nx + d) for d in range(nx)], w_own)
+
+    def line(v):
+        v = jnp.sum(jnp.sum(v, axis=0, keepdims=True), axis=1, keepdims=True)
+        return jnp.broadcast_to(v, (1, 128))
 
     red_z[z] = jnp.zeros((8, 128), F32)
-    red_z[z, 0:1, :] = jnp.broadcast_to(jnp.sum(part, axis=1, keepdims=True) * math.log(2.0), (1, 128))
-    red_z[z, 1:2, :] = jnp.broadcast_to(jnp.sum(row_0[3], axis=1, keepdims=True), (1, 128))
+    red_z[z, 0:1, :] = line(part) * math.log(2.0)
+    red_z[z, 1:2, :] = line(w_own)
 
     def z_copy(source, to):
         return pltpu.make_async_remote_copy(
@@ -334,14 +350,30 @@
     def _():
         greet(ready, other_group)
 
+    def exponent(ref, at, count, w):
+        ms, ls = (
+            [ref[d, (q * count + at[d]) * per : (q * count + at[d] + 1) * per, :] for d in range(count)]
+            for q in range(2)
+        )
+        m = functools.reduce(jnp.maximum, ms)
+        l = sum(li * jnp.exp2(mi - m) for mi, li in zip(ms, ls))
+        return m + jnp.log2(l / w)
+
+    for c in cs_copies:
+        c.wait_recv()
+    b_rows = []
     for b in range(nyc):
-        m, l, _, w = column_stats(b) if b else column_0
-        brow[0:1, b * n : (b + 1) * n] = m + jnp.log2(l / w)
+        at = [b ^ d for d in range(nyc)]
+        w = sum(colst[d, (2 * nyc + at[d]) * per : (2 * nyc + at[d] + 1) * per, :] for d in range(nyc))
+        v = exponent(colst, at, nyc, w)
+        b_rows += [v[h : h + 1, :] for h in range(per)]
+    for c in rs_copies:
+        c.wait_recv()
     for r in (2, 1, 3, 0):
-        m, l, _, w = row_stats(r) if r else row_0
-        acol[r * n : (r + 1) * n, :] = jnp.broadcast_to(m + jnp.log2(l / w), (128, n)).T
-
-    b_rows = [brow[0:1, c * 128 : (c + 1) * 128] for c in range(chunks)]
+        w = jnp.concatenate([wp[r, 0:1, h * 128 : (h + 1) * 128] for h in range(per)], axis=0)
+        a = exponent(rowst, [(r - d) % nx for d in range(nx)], nx, w)
+        for h in range(per):
+            acol[r * n + h * 128 : r * n + (h + 1) * 128, :] = jnp.broadcast_to(a[h : h + 1, :], (128, 128)).T
 
     def gradients(slot):
         def step(i, carry):
@@ -408,9 +440,9 @@
     gu_r1.wait_recv()
     gu_r0.wait_recv()
     gu_l1.wait_recv()
-    own_gu[...] = own_gu[...] + from_left[...].astype(F32) + from_right[...].astype(F32)
+    gu_out[...] = own_gu[...] + from_left[...].astype(F32) + from_right[...].astype(F32)
     gi_y.wait_recv()
-    own_gi[...] = own_gi[...] + from_y[...].astype(F32)
+    gi_out[...] = own_gi[...] + from_y[...].astype(F32)
 
     def plane_copy(source, to):
         return pltpu.make_async_remote_copy(
@@ -441,26 +473,31 @@
         loop(here + 1, 2 * n_blk, lambda source: plane_copy(source, source).wait_recv())
         totals[...] = jnp.sum(red_plane[...], axis=0)
         loop(1, depth, lambda to: all_copy(to).start())
+
+    @pl.when(z > 0)
+    def _():
+        all_copy(0).wait_recv()
+
+    sums = totals[...]
+    weight = sums[1:2, :]
+    scale_out[...] = jnp.broadcast_to(sums[0:1, :] / weight, (8, 128))
+    rows_total = float(n * n_blk * n_dp)
+    factor = (rows_total / weight) * (k[:, 0:128] * math.log(2.0))
+    factor_out[...] = jnp.concatenate([factor] * (width // 128), axis=1)
+
+    for c in started:
+        c.wait_send()
+
+    @pl.when(z > 0)
+    def _():
+        z_copy(z, 0).wait_send()
+
+    @pl.when(z == 0)
+    def _():
+        here = high * n_blk + me
         loop(0, here, lambda to: plane_copy(here, to).wait_send())
         loop(here + 1, 2 * n_blk, lambda to: plane_copy(here, to).wait_send())
         loop(1, depth, lambda to: all_copy(to).wait_send())
-
-    @pl.when(z > 0)
-    def _():
-        all_copy(0).wait_recv()
-        z_copy(z, 0).wait_send()
-
-    sums = totals[...]
-    weight = sums[1:2, :]
-    scale_out[0] = (sums[0:1, :] / weight)[0, 0]
-    rows_total = float(n * n_blk * n_dp)
-    factor = (rows_total / weight) * (k[:, 0:128] * math.log(2.0))
-    factor = jnp.concatenate([factor] * (width // 128), axis=1)
-    gu_out[...] = (factor * own_gu[...]).astype(BF16)
-    gi_out[...] = (factor * own_gi[...]).astype(BF16)
-
-    for c in started:
-        c.wait_send()
 
 
 def body(users, items, weights, positives, log_scale):
@@ -471,19 +508,19 @@
     nx = n_blk // nyc
     any_space = pl.BlockSpec(memory_space=pl.ANY)
     vmem = pl.BlockSpec(memory_space=pltpu.VMEM)
-    smem = pl.BlockSpec(memory_space=pltpu.SMEM)
     V = pltpu.VMEM
     rows, cols = nx * n, nyc * n
     half = n // 2
-    gu, gi, scale = pl.pallas_call(
+    gu, gi, scale, factor = pl.pallas_call(
         functools.partial(kernel, nx, nyc, n_dp, n_blk),
         out_shape=(
-            pltpu.VMEM((n, width), BF16),
-            pltpu.VMEM((n, width), BF16),
-            jax.ShapeDtypeStruct((1,), F32),
+            V((n, width), F32),
+            V((n, width), F32),
+            V((8, 128), F32),
+            V((1, width), F32),
         ),
-        in_specs=[any_space, any_space, any_space, any_space, smem],
-        out_specs=(vmem, vmem, smem),
+        in_specs=[any_space] * 5,
+        out_specs=(vmem,) * 4,
         scratch_shapes=[
             V((rows, width), BF16),
             V((cols, width), BF16),
@@ -497,9 +534,11 @@
             V((rows, 128), F32),
             V((n, 128), F32),
             V((3, n, 128), F32),
-            V((nx, 16, n), F32),
-            V((nyc, 24, n), F32),
-            V((8, cols), F32),
+            V((nx, 2 * nx * n // 128, 128), F32),
+            V((nyc, 3 * nyc * n // 128, 128), F32),
+            V((2 * nx, 8, 128), F32),
+            V((2 * nyc, 16, 128), F32),
+            pltpu.SMEM((1,), F32),
             V((n, width), BF16),
             V((half, width), BF16),
             V((half, width), BF16),
@@ -519,7 +558,7 @@
             V((n_dp // 2, 8, 128), F32),
             V((2 * n_blk, 8, 128), F32),
             V((8, 128), F32),
-            pltpu.SemaphoreType.DMA((4,)),
+            pltpu.SemaphoreType.DMA((5,)),
             pltpu.SemaphoreType.DMA((TRANSFERS,)),
             pltpu.SemaphoreType.DMA((TRANSFERS,)),
             pltpu.SemaphoreType.DMA((1,)),
@@ -539,7 +578,7 @@
         ),
         name="loss_gradients",
     )(users, items, weights, positives, log_scale)
-    return gu[None], gi[None], scale
+    return (gu * factor).astype(BF16)[None], (gi * factor).astype(BF16)[None], scale[0, 0:1]
 
 
 def solution(mesh):

time: 51 us -> 49.2 us (0.965)
  between operations: 2.98 us -> 1.29 us
  other arithmetic: 0 us -> 0.91 us
  local copies, waits for them, and re-layouts: 1.41 us -> 0.51 us
    unnamed x2 -> x0, local copies, waits for them, and re-layouts: 1.41 us -> none
    broadcast_in_dim x0 -> x1, other arithmetic: none -> 0.91 us  [body(): (gi * factor).astype(BF16)[None]]
    slice x0 -> x1, local copies, waits for them, and re-layouts: none -> 0.51 us  [body(): scale[0, 0:1]]
where the time goes in v4:
time: 49.2 us; the launch traced here: 49.1 us
  Pallas kernels  46.4 us (94%)
  between operations  1.29 us (3%)
  other arithmetic  0.91 us (2%)
  local copies, waits for them, and re-layouts  0.51 us (1%)
    pallas_call x1, Pallas kernels, body(): pl.pallas_call(functools.partial(kernel, nx, nyc, n_dp, n_blk), out_shape...  46.4 us

profile of v4, /device:TPU:1, one launch (start us, length us, event | category | flops | bytes accessed | tf_op | source)
XLA Modules:
  0.0 49.1 jit_solution(1617745346038062894)
XLA Ops:
  1.3 46.4 %loss_gradients.1 = (f32[256,512]{1,0:T(8,128)S(1)}, f32[256,512]{1,0:T(8,128)S(1)}, f32[8,128]{1,0:T(8,128)S(1)}, f32[1,512]{1,0:T(1,128)S(1)}) custom-call(bf16[256,512]{1,0:T(8,128)(2,1)} %bitcast.9, bf16[256,512]{1,0:T(8,128)(2,1)} %bitcast.10, f32[1,256]{1,0:T(1,128)} %weights.1, s32[1,256]{1,0:T(1,128)} %positives.1, f32[1]{0:T(128)S(6)} %copy.8.log_scale), custom_call_target="tpu_custom_call" | custom-call | flops 3221225472 | bytes 1048576 | tf_op jit(solution)/shard_map/loss_gradients/pallas_call | solution.py:514
  47.7 0.5 %slice.3 = f32[1,1]{1,0:T(1,128)} slice(f32[8,128]{1,0:T(8,128)S(1)} %get-tuple-element.10), slice={[0:1], [0:1]} | slice | bytes 8 | tf_op jit(solution)/shard_map/slice | solution.py:581
  48.2 0.9 %fusion.1 = (bf16[1,256,512]{2,1,0:T(8,128)(2,1)}, bf16[1,256,512]{2,1,0:T(8,128)(2,1)}) fusion(f32[256,512]{1,0:T(8,128)S(1)} %get-tuple-element.9, f32[512]{0:T(512)S(1)} %bitcast.8, f32[256,512]{1,0:T(8,128)S(1)} %get-tuple-element.7), kind=kLoop, calls=%fused_computation.3 | loop fusion | flops 524288 | bytes 1574912 | tf_op jit(solution)/shard_map/broadcast_in_dim | solution.py:581

commit v5 on v4

--- a/solution.py
+++ b/solution.py
@@ -17,11 +17,11 @@
 (
     U_RIGHT_0, U_LEFT_1, U_RIGHT_1, U_LEFT_0, U_RELAY_RIGHT, U_RELAY_LEFT,
     I_CORE, I_Y, I_Y_1, I_Y_2, I_Y_3, I_PASS, I_PASS_1, I_PASS_2, I_PASS_3,
-    WP_RIGHT, WP_LEFT, WP_RELAY, RS_1, RS_2, RS_3, CS_1, CS_2, CS_3, RO_1, RO_2, RO_3, CO_1, CO_2, CO_3,
+    WP_RIGHT, WP_LEFT, WP_RELAY, RS_1, RS_2, RS_3, CS_1, CS_2, CS_3,
     GU_FAR_RIGHT, GU_FAR_LEFT, GU_RIGHT_0, GU_RIGHT_1, GU_LEFT_0, GU_LEFT_1,
     GI_CORE_0, GI_CORE_1, GI_Y,
     TRANSFERS,
-) = range(40)
+) = range(34)
 
 
 def dot_nt(a, b):
@@ -44,11 +44,11 @@
     users, items, weights, positives, log_scale,
     gu_out, gi_out, scale_out, factor_out,
     u_all, i_all, w_in, p_in, wp, t_all, g_all, wcol, pcol, acol, row_m, lines,
-    rowst, colst, row_own, col_own, log_in,
+    rowst, colst, log_in,
     far, far_right, far_left, to_left, to_right, from_left, from_right,
     own_gu, own_gi, other_gi, core_0, core_1, got_core_0, got_core_1, to_y, from_y,
-    red_z, red_plane, totals,
-    local_sem, send, recv, z_send, z_recv, plane_send, plane_recv, all_send, all_recv, ready,
+    mine, parts_in, totals,
+    local_sem, send, recv, part_send, part_recv, all_send, all_recv, hello, ready, go,
 ):
     n = users.shape[0]
     width = users.shape[1]
@@ -78,10 +78,16 @@
     def at_z(to):
         return {"blk": me, "dp": high * depth + to}
 
-    def at_plane(p):
-        return {"blk": p % n_blk, "dp": (p // n_blk) * depth}
-
-    other_group = {"blk": me, "dp": (1 - high) * depth + z}
+    def at_plane(r):
+        if r < 8:
+            flip, dx, c = r % 4, 0, (1 - core if r >= 4 else core)
+        else:
+            flip, dx, c = (r - 8) // 3, (r - 8) % 3 + 1, core
+        w = 1 - y if flip in (1, 2) else y
+        v = 1 - high if flip in (1, 3) else high
+        return {"blk": ((x + dx) % nx) * nyc + w * 2 + c, "dp": v * depth}
+
+    next_y = at_plane(1)
 
     right, left = at_x(1), at_x(nx - 1)
 
@@ -125,10 +131,9 @@
 
         @pl.when(high == 0)
         def _():
-            greet(barrier, other_group)
+            greet(barrier, next_y)
 
     wp[0] = jnp.zeros((8, n), F32)
-    col_own[0:nyc] = jnp.zeros((nyc, 16, 128), F32)
     pl.semaphore_wait(barrier, 4 + jnp.where(my_dp == 0, 0, 1))
 
     def u_rows(slot, h):
@@ -166,6 +171,10 @@
     u_l0 = start(remote(piece(users, 0), u_rows(3, 0), U_LEFT_0, left))
     for c in locals_[2:]:
         c.wait()
+
+    @pl.when(z > 0)
+    def _():
+        greet(hello, at_z(0))
 
     k = jnp.exp(jnp.full((1, 2 * n), log_in[0], F32)) * (1.0 / (math.sqrt(width) * math.log(2.0)))
 
@@ -238,11 +247,8 @@
         row = [row_m[...].T[0:1, :]] + [jnp.sum(lines[q].T, axis=0, keepdims=True) for q in range(3)]
         for q in range(4):
             for h in range(per):
-                v = row[q][:, h * 128 : (h + 1) * 128]
-                row_own[nx - slot, q * per + h : q * per + h + 1, :] = v
-                if q < 2:
-                    at = (q * nx + slot) * per + h
-                    rowst[0, at : at + 1, :] = v
+                at = (q * nx + slot) * per + h
+                rowst[0, at : at + 1, :] = row[q][:, h * 128 : (h + 1) * 128]
         return best, total
 
     parts = {}
@@ -281,97 +287,117 @@
     for slot in (0, 1, 3):
         scores(slot, 3, 4)
         parts[slot] = statistics(slot)
+    def of_slot(s, c):
+        return (parts[s][0][c],) + tuple(parts[s][1][4 * c : 4 * c + 4])
+
+    def join(one, two):
+        m = jnp.maximum(one[0], two[0])
+        l = e = 0.0
+        for v in (one, two):
+            scale = jnp.exp2(v[0] - m)
+            l = l + scale * v[1]
+            e = e + scale * (v[2] + (v[0] - m) * v[1])
+        return m, l, e, one[3] + two[3], one[4] + two[4]
+
+    early = [join(join(of_slot(0, c), of_slot(1, c)), of_slot(3, c)) for c in range(chunks)]
     relay_r.wait_recv()
     relay_l.wait_recv()
     scores(2, 0, 4)
     parts[2] = statistics(2)
 
-    ro_copies = [start(remote(row_own.at[d], row_own.at[nx + d], RO_1 + d - 1, at_x(d))) for d in (2, 1, 3)]
+    rs_copies = [start(remote(rowst.at[0], rowst.at[d], RS_1 + d - 1, at_x(d))) for d in (2, 1, 3)]
+    joined = [join(early[c], of_slot(2, c)) for c in range(chunks)]
     for c in range(chunks):
         b, h = c // per, c % per
-        ms = [parts[s][0][c] for s in range(nx)]
-        m = functools.reduce(jnp.maximum, ms)
-        l = e = 0.0
-        for s in range(nx):
-            scale = jnp.exp2(ms[s] - m)
-            part_l = parts[s][1][4 * c]
-            l = l + scale * part_l
-            e = e + scale * (parts[s][1][4 * c + 1] + (ms[s] - m) * part_l)
-        hit = sum(parts[s][1][4 * c + 2] for s in range(nx))
-        cw = sum(parts[s][1][4 * c + 3] for s in range(nx))
-        for q, v in enumerate((m, l, e, hit, cw)):
-            col_own[b, q * per + h : q * per + h + 1, :] = v
-        for q, v in enumerate((m, l, cw)):
+        for q, v in enumerate(joined[c]):
             at = (q * nyc + b) * per + h
             colst[0, at : at + 1, :] = v
-    co_copies = [start(remote(col_own.at[d], col_own.at[nyc + d], CO_1 + d - 1, at_yc(d))) for d in (3, 2, 1)]
-    rs_copies = [start(remote(rowst.at[0], rowst.at[d], RS_1 + d - 1, at_x(d))) for d in (2, 1, 3)]
     cs_copies = [start(remote(colst.at[0], colst.at[d], CS_1 + d - 1, at_yc(d))) for d in (3, 2, 1)]
 
-    def total_share(sources, w):
-        ms, ls, es, hits = ([src(q) for src in sources] for q in range(4))
+    @pl.when(z == 0)
+    def _():
+        @pl.when(high == 1)
+        def _():
+            greet(ready, next_y)
+
+        pl.semaphore_wait(ready, 1)
+
+        @pl.when(high == 0)
+        def _():
+            greet(ready, next_y)
+
+        pl.semaphore_wait(hello, depth - 1)
+        loop(1, depth, lambda to: greet(go, at_z(to)))
+
+    def combine(ref, at, count, w):
+        ms, ls, es, hits = (
+            [ref[d, (q * count + at[d]) * per : (q * count + at[d] + 1) * per, :] for d in range(count)]
+            for q in range(4)
+        )
         m = functools.reduce(jnp.maximum, ms)
         scales = [jnp.exp2(mi - m) for mi in ms]
         l = sum(li * si for li, si in zip(ls, scales))
         e = sum(si * (ei + (mi - m) * li) for mi, li, ei, si in zip(ms, ls, es, scales))
-        return w * (e / l - (sum(hits) - m))
-
-    def own_rows(ref, i):
-        return lambda q: ref[i, q * per : (q + 1) * per, :]
-
-    for c in co_copies:
+        return m, l, w * (e / l - (sum(hits) - m))
+
+    for c in cs_copies:
         c.wait_recv()
-    columns = [own_rows(col_own, i) for i in [0] + [nyc + d for d in range(1, nyc)]]
-    part = total_share(columns, sum(src(4) for src in columns))
-    for c in ro_copies:
+    columns = []
+    for b in range(nyc):
+        at = [b ^ d for d in range(nyc)]
+        w = sum(colst[d, (4 * nyc + at[d]) * per : (4 * nyc + at[d] + 1) * per, :] for d in range(nyc))
+        columns.append(combine(colst, at, nyc, w) + (w,))
+    w_rows = [
+        jnp.concatenate([wp[r, 0:1, h * 128 : (h + 1) * 128] for h in range(per)], axis=0) for r in range(nx)
+    ]
+    for c in rs_copies:
         c.wait_recv()
-    w_own = jnp.concatenate([wp[0, 0:1, h * 128 : (h + 1) * 128] for h in range(per)], axis=0)
-    part = part + total_share([own_rows(row_own, nx + d) for d in range(nx)], w_own)
+    rows_ = [combine(rowst, [(r - d) % nx for d in range(nx)], nx, w_rows[r]) + (w_rows[r],) for r in range(nx)]
 
     def line(v):
         v = jnp.sum(jnp.sum(v, axis=0, keepdims=True), axis=1, keepdims=True)
         return jnp.broadcast_to(v, (1, 128))
 
-    red_z[z] = jnp.zeros((8, 128), F32)
-    red_z[z, 0:1, :] = line(part) * math.log(2.0)
-    red_z[z, 1:2, :] = line(w_own)
-
-    def z_copy(source, to):
+    first_half = lane < 64
+    row_line = jnp.where(first_half, line(sum(v[2] for v in rows_)) * math.log(2.0), line(sum(w_rows)))
+    column_line = jnp.where(first_half, line(sum(v[2] for v in columns)) * math.log(2.0), 0.0)
+    mine[0] = row_line + column_line
+    mine[1] = row_line
+    mine[2] = column_line
+
+    relations = 14
+
+    def part_copy(r):
         return pltpu.make_async_remote_copy(
-            src_ref=red_z.at[source], dst_ref=red_z.at[source], send_sem=z_send.at[0],
-            recv_sem=z_recv.at[source], device_id=at_z(to), device_id_type=MESH,
-        )
+            src_ref=mine.at[0 if r < 2 else 1 if r < 8 else 2], dst_ref=parts_in.at[z * relations + r],
+            send_sem=part_send.at[r], recv_sem=part_recv.at[0], device_id=at_plane(r), device_id_type=MESH,
+        )
+
+    own_part = pltpu.make_async_copy(mine.at[0], parts_in.at[0], part_recv.at[0])
+    others = (11, 12, 13, 8, 9, 10, 5, 6, 7, 1, 2, 3, 4)
 
     @pl.when(z > 0)
     def _():
-        z_copy(z, 0).start()
-
-    @pl.when((z == 0) & (high == 1))
-    def _():
-        greet(ready, other_group)
-
-    def exponent(ref, at, count, w):
-        ms, ls = (
-            [ref[d, (q * count + at[d]) * per : (q * count + at[d] + 1) * per, :] for d in range(count)]
-            for q in range(2)
-        )
-        m = functools.reduce(jnp.maximum, ms)
-        l = sum(li * jnp.exp2(mi - m) for mi, li in zip(ms, ls))
-        return m + jnp.log2(l / w)
-
-    for c in cs_copies:
-        c.wait_recv()
+        pl.semaphore_wait(go, 1)
+        part_copy(12).start()
+        part_copy(0).start()
+
+    @pl.when(z == 0)
+    def _():
+        own_part.start()
+        part_copy(12).start()
+
+    for r in others:
+        if r != 12:
+            part_copy(r).start()
+
     b_rows = []
-    for b in range(nyc):
-        at = [b ^ d for d in range(nyc)]
-        w = sum(colst[d, (2 * nyc + at[d]) * per : (2 * nyc + at[d] + 1) * per, :] for d in range(nyc))
-        v = exponent(colst, at, nyc, w)
+    for m, l, _, w in columns:
+        v = m + jnp.log2(l / w)
         b_rows += [v[h : h + 1, :] for h in range(per)]
-    for c in rs_copies:
-        c.wait_recv()
     for r in (2, 1, 3, 0):
-        w = jnp.concatenate([wp[r, 0:1, h * 128 : (h + 1) * 128] for h in range(per)], axis=0)
-        a = exponent(rowst, [(r - d) % nx for d in range(nx)], nx, w)
+        m, l, _, w = rows_[r]
+        a = m + jnp.log2(l / w)
         for h in range(per):
             acol[r * n + h * 128 : r * n + (h + 1) * 128, :] = jnp.broadcast_to(a[h : h + 1, :], (128, 128)).T
 
@@ -444,11 +470,14 @@
     gi_y.wait_recv()
     gi_out[...] = own_gi[...] + from_y[...].astype(F32)
 
-    def plane_copy(source, to):
-        return pltpu.make_async_remote_copy(
-            src_ref=red_plane.at[source], dst_ref=red_plane.at[source], send_sem=plane_send.at[to],
-            recv_sem=plane_recv.at[source], device_id=at_plane(to), device_id_type=MESH,
-        )
+    for c in started:
+        c.wait_send()
+    for r in others:
+        part_copy(r).wait_send()
+
+    @pl.when(z > 0)
+    def _():
+        part_copy(0).wait_send()
 
     def all_copy(to):
         return pltpu.make_async_remote_copy(
@@ -458,20 +487,11 @@
 
     @pl.when(z == 0)
     def _():
-        here = high * n_blk + me
-        pl.semaphore_wait(ready, 1)
-
-        @pl.when(high == 0)
-        def _():
-            greet(ready, other_group)
-
-        loop(1, depth, lambda source: z_copy(source, 0).wait_recv())
-        red_plane[here] = jnp.sum(red_z[...], axis=0)
-        loop(0, here, lambda to: plane_copy(here, to).start())
-        loop(here + 1, 2 * n_blk, lambda to: plane_copy(here, to).start())
-        loop(0, here, lambda source: plane_copy(source, source).wait_recv())
-        loop(here + 1, 2 * n_blk, lambda source: plane_copy(source, source).wait_recv())
-        totals[...] = jnp.sum(red_plane[...], axis=0)
+        pltpu.make_async_copy(parts_in, parts_in, part_recv.at[0]).wait()
+        sums = [parts_in[i] for i in range(relations * depth)]
+        while len(sums) > 1:
+            sums = [sum(sums[i : i + 2]) for i in range(0, len(sums), 2)]
+        totals[...] = sums[0]
         loop(1, depth, lambda to: all_copy(to).start())
 
     @pl.when(z > 0)
@@ -479,24 +499,14 @@
         all_copy(0).wait_recv()
 
     sums = totals[...]
-    weight = sums[1:2, :]
-    scale_out[...] = jnp.broadcast_to(sums[0:1, :] / weight, (8, 128))
+    weight = jnp.broadcast_to(sums[:, 64:65], (1, 128))
+    scale_out[...] = jnp.broadcast_to(sums[:, 0:1] / weight, (8, 128))
     rows_total = float(n * n_blk * n_dp)
     factor = (rows_total / weight) * (k[:, 0:128] * math.log(2.0))
     factor_out[...] = jnp.concatenate([factor] * (width // 128), axis=1)
 
-    for c in started:
-        c.wait_send()
-
-    @pl.when(z > 0)
-    def _():
-        z_copy(z, 0).wait_send()
-
     @pl.when(z == 0)
     def _():
-        here = high * n_blk + me
-        loop(0, here, lambda to: plane_copy(here, to).wait_send())
-        loop(here + 1, 2 * n_blk, lambda to: plane_copy(here, to).wait_send())
         loop(1, depth, lambda to: all_copy(to).wait_send())
 
 
@@ -534,10 +544,8 @@
             V((rows, 128), F32),
             V((n, 128), F32),
             V((3, n, 128), F32),
-            V((nx, 2 * nx * n // 128, 128), F32),
-            V((nyc, 3 * nyc * n // 128, 128), F32),
-            V((2 * nx, 8, 128), F32),
-            V((2 * nyc, 16, 128), F32),
+            V((nx, 4 * nx * n // 128, 128), F32),
+            V((nyc, 5 * nyc * n // 128, 128), F32),
             pltpu.SMEM((1,), F32),
             V((n, width), BF16),
             V((half, width), BF16),
@@ -555,18 +563,18 @@
             V((n, width), BF16),
             V((n, width), BF16),
             V((n, width), BF16),
-            V((n_dp // 2, 8, 128), F32),
-            V((2 * n_blk, 8, 128), F32),
-            V((8, 128), F32),
+            V((3, 1, 128), F32),
+            V((14 * n_dp // 2, 1, 128), F32),
+            V((1, 128), F32),
             pltpu.SemaphoreType.DMA((5,)),
             pltpu.SemaphoreType.DMA((TRANSFERS,)),
             pltpu.SemaphoreType.DMA((TRANSFERS,)),
+            pltpu.SemaphoreType.DMA((14,)),
             pltpu.SemaphoreType.DMA((1,)),
             pltpu.SemaphoreType.DMA((n_dp // 2,)),
-            pltpu.SemaphoreType.DMA((2 * n_blk,)),
-            pltpu.SemaphoreType.DMA((2 * n_blk,)),
-            pltpu.SemaphoreType.DMA((n_dp // 2,)),
             pltpu.SemaphoreType.DMA((1,)),
+            pltpu.SemaphoreType.REGULAR,
+            pltpu.SemaphoreType.REGULAR,
             pltpu.SemaphoreType.REGULAR,
         ],
         compiler_params=pltpu.CompilerParams(

time: 49.2 us -> 45.5 us (0.925)
  the two profiles are of different devices: /device:TPU:1 before, /device:TPU:32 now
where the time goes in v5:
time: 45.5 us; the launch traced here: 45.3 us
  Pallas kernels  42.6 us (94%)
  between operations  1.29 us (3%)
  other arithmetic  0.91 us (2%)
  local copies, waits for them, and re-layouts  0.51 us (1%)
    pallas_call x1, Pallas kernels, body(): pl.pallas_call(functools.partial(kernel, nx, nyc, n_dp, n_blk), out_shape...  42.6 us

profile of v5, /device:TPU:32, one launch (start us, length us, event | category | flops | bytes accessed | tf_op | source)
XLA Modules:
  0.0 45.3 jit_solution(12856884449073277862)
XLA Ops:
  1.3 42.6 %loss_gradients.1 = (f32[256,512]{1,0:T(8,128)S(1)}, f32[256,512]{1,0:T(8,128)S(1)}, f32[8,128]{1,0:T(8,128)S(1)}, f32[1,512]{1,0:T(1,128)S(1)}) custom-call(bf16[256,512]{1,0:T(8,128)(2,1)} %bitcast.9, bf16[256,512]{1,0:T(8,128)(2,1)} %bitcast.10, f32[1,256]{1,0:T(1,128)} %weights.1, s32[1,256]{1,0:T(1,128)} %positives.1, f32[1]{0:T(128)S(6)} %copy.8.log_scale), custom_call_target="tpu_custom_call" | custom-call | flops 3221225472 | bytes 1048576 | tf_op jit(solution)/shard_map/loss_gradients/pallas_call | solution.py:524
  43.9 0.5 %slice.3 = f32[1,1]{1,0:T(1,128)} slice(f32[8,128]{1,0:T(8,128)S(1)} %get-tuple-element.10), slice={[0:1], [0:1]} | slice | bytes 8 | tf_op jit(solution)/shard_map/slice | solution.py:589
  44.4 0.9 %fusion.1 = (bf16[1,256,512]{2,1,0:T(8,128)(2,1)}, bf16[1,256,512]{2,1,0:T(8,128)(2,1)}) fusion(f32[256,512]{1,0:T(8,128)S(1)} %get-tuple-element.9, f32[512]{0:T(512)S(1)} %bitcast.8, f32[256,512]{1,0:T(8,128)S(1)} %get-tuple-element.7), kind=kLoop, calls=%fused_computation.3 | loop fusion | flops 524288 | bytes 1574912 | tf_op jit(solution)/shard_map/broadcast_in_dim | solution.py:589

commit v6 on v5

--- a/solution.py
+++ b/solution.py
@@ -19,9 +19,9 @@
     I_CORE, I_Y, I_Y_1, I_Y_2, I_Y_3, I_PASS, I_PASS_1, I_PASS_2, I_PASS_3,
     WP_RIGHT, WP_LEFT, WP_RELAY, RS_1, RS_2, RS_3, CS_1, CS_2, CS_3,
     GU_FAR_RIGHT, GU_FAR_LEFT, GU_RIGHT_0, GU_RIGHT_1, GU_LEFT_0, GU_LEFT_1,
-    GI_CORE_0, GI_CORE_1, GI_Y,
+    GI_CORE_0, GI_CORE_1, GI_Y, RX_0, RX_1, RX_2, RX_3, WX,
     TRANSFERS,
-) = range(34)
+) = range(39)
 
 
 def dot_nt(a, b):
@@ -44,7 +44,7 @@
     users, items, weights, positives, log_scale,
     gu_out, gi_out, scale_out, factor_out,
     u_all, i_all, w_in, p_in, wp, t_all, g_all, wcol, pcol, acol, row_m, lines,
-    rowst, colst, log_in,
+    rowst, other_rowst, other_w, colst, cpart, fold, w_rows, a_rows, b_tile, log_in,
     far, far_right, far_left, to_left, to_right, from_left, from_right,
     own_gu, own_gi, other_gi, core_0, core_1, got_core_0, got_core_1, to_y, from_y,
     mine, parts_in, totals,
@@ -75,17 +75,14 @@
         w = 1 - y if d // 2 else y
         return {"blk": x * nyc + w * 2 + c, "dp": my_dp}
 
-    def at_z(to):
-        return {"blk": me, "dp": high * depth + to}
+    def at_z(to, c=1):
+        return {"blk": x * nyc + y * 2 + c, "dp": high * depth + to}
 
     def at_plane(r):
-        if r < 8:
-            flip, dx, c = r % 4, 0, (1 - core if r >= 4 else core)
-        else:
-            flip, dx, c = (r - 8) // 3, (r - 8) % 3 + 1, core
+        flip, dx = (r, 0) if r < 4 else ((r - 4) // 3, (r - 4) % 3 + 1)
         w = 1 - y if flip in (1, 2) else y
         v = 1 - high if flip in (1, 3) else high
-        return {"blk": ((x + dx) % nx) * nyc + w * 2 + c, "dp": v * depth}
+        return {"blk": ((x + dx) % nx) * nyc + w * 2 + 1, "dp": v * depth}
 
     next_y = at_plane(1)
 
@@ -125,7 +122,7 @@
     for c in locals_:
         c.start()
 
-    @pl.when(z == 0)
+    @pl.when((z == 0) & (core == 1))
     def _():
         loop(1, depth, lambda to: greet(barrier, at_z(to)))
 
@@ -134,7 +131,7 @@
             greet(barrier, next_y)
 
     wp[0] = jnp.zeros((8, n), F32)
-    pl.semaphore_wait(barrier, 4 + jnp.where(my_dp == 0, 0, 1))
+    pl.semaphore_wait(barrier, 4 + jnp.where((core == 0) | (my_dp == 0), 0, 1))
 
     def u_rows(slot, h):
         return u_all.at[pl.ds(slot * n + h * half, half)]
@@ -172,7 +169,7 @@
     for c in locals_[2:]:
         c.wait()
 
-    @pl.when(z > 0)
+    @pl.when((z > 0) & (core == 1))
     def _():
         greet(hello, at_z(0))
 
@@ -194,11 +191,19 @@
 
     ids = [column_ids(c) for c in range(chunks)]
 
+    def row_place(slot, h):
+        return ((x + nx - slot) % nx) * per + h
+
+    def column_place(c):
+        return (at_yc(c // per)["blk"] % nyc) * per + c % per
+
     def spread(slot):
+        for h in range(per):
+            w_rows[pl.ds(row_place(slot, h), 1), :] = wp[slot, 0:1, h * 128 : (h + 1) * 128]
         wcol[slot * n : (slot + 1) * n, :] = jnp.broadcast_to(wp[slot, 0:1, :], (128, n)).T
         pcol[slot * n : (slot + 1) * n, :] = jnp.broadcast_to(wp[slot, 1:2, :], (128, n)).T
 
-    def statistics(slot):
+    def statistics(slot, rows_done=lambda: None):
         def maxima(i, best):
             rows = pl.ds(pl.multiple_of(slot * n + i * CHUNK, CHUNK), CHUNK)
             top = None
@@ -243,15 +248,20 @@
         total = lax.fori_loop(
             0, steps, sums, tuple(jnp.zeros((8, 128), F32) for _ in range(4 * chunks)), unroll=True
         )
-        total = [jnp.sum(b, axis=0, keepdims=True) for b in total]
         row = [row_m[...].T[0:1, :]] + [jnp.sum(lines[q].T, axis=0, keepdims=True) for q in range(3)]
         for q in range(4):
             for h in range(per):
-                at = (q * nx + slot) * per + h
-                rowst[0, at : at + 1, :] = row[q][:, h * 128 : (h + 1) * 128]
-        return best, total
-
-    parts = {}
+                rowst[0, pl.ds(q * nx * per + row_place(slot, h), 1), :] = row[q][:, h * 128 : (h + 1) * 128]
+        rows_done()
+        for c in range(chunks):
+            cpart[slot, pl.ds(column_place(c), 1), :] = best[c]
+            for q in range(4):
+                fold[q, pl.ds(pl.multiple_of(column_place(c) * 8, 8), 8), :] = total[4 * c + q]
+        for q in range(4):
+            cpart[slot, (q + 1) * chunks : (q + 2) * chunks, :] = sum(
+                fold[q, pl.ds(r, chunks, stride=8), :] for r in range(8)
+            )
+
     spread(0)
     i_core.wait_recv()
     scores(0, 0, 2)
@@ -275,6 +285,12 @@
     pass_on(1)
     wp_relay.wait_recv()
     spread(2)
+    weights_copy = remote(w_rows, other_w, WX, at_yc(1))
+
+    @pl.when(core == 0)
+    def _():
+        weights_copy.start()
+
     pass_on(2)
     pass_on(3)
     scores(0, 2, 3)
@@ -286,9 +302,9 @@
         c.wait_recv()
     for slot in (0, 1, 3):
         scores(slot, 3, 4)
-        parts[slot] = statistics(slot)
-    def of_slot(s, c):
-        return (parts[s][0][c],) + tuple(parts[s][1][4 * c : 4 * c + 4])
+        statistics(slot)
+    def of_slot(s):
+        return [cpart[s, q * chunks : (q + 1) * chunks, :] for q in range(5)]
 
     def join(one, two):
         m = jnp.maximum(one[0], two[0])
@@ -299,22 +315,56 @@
             e = e + scale * (v[2] + (v[0] - m) * v[1])
         return m, l, e, one[3] + two[3], one[4] + two[4]
 
-    early = [join(join(of_slot(0, c), of_slot(1, c)), of_slot(3, c)) for c in range(chunks)]
+    early = join(join(of_slot(0), of_slot(1)), of_slot(3))
     relay_r.wait_recv()
     relay_l.wait_recv()
     scores(2, 0, 4)
-    parts[2] = statistics(2)
-
-    rs_copies = [start(remote(rowst.at[0], rowst.at[d], RS_1 + d - 1, at_x(d))) for d in (2, 1, 3)]
-    joined = [join(early[c], of_slot(2, c)) for c in range(chunks)]
-    for c in range(chunks):
-        b, h = c // per, c % per
-        for q, v in enumerate(joined[c]):
-            at = (q * nyc + b) * per + h
-            colst[0, at : at + 1, :] = v
-    cs_copies = [start(remote(colst.at[0], colst.at[d], CS_1 + d - 1, at_yc(d))) for d in (3, 2, 1)]
-
-    @pl.when(z == 0)
+    def to_core_1(d):
+        return remote(
+            rowst.at[0], other_rowst.at[d], RX_0 + d, {"blk": ((x + d) % nx) * nyc + y * 2 + 1, "dp": my_dp}
+        )
+
+    def send_rows():
+        @pl.when(core == 0)
+        def _():
+            for d in (2, 1, 3, 0):
+                to_core_1(d).start()
+            for d in (2, 1, 3):
+                row_copy(d, 2).start()
+
+        @pl.when(core == 1)
+        def _():
+            for d in (2, 1, 3):
+                row_copy(d, 4).start()
+
+    def row_copy(d, count):
+        size = count * nx * per
+        return remote(rowst.at[0, pl.ds(0, size)], rowst.at[d, pl.ds(0, size)], RS_1 + d - 1, at_x(d))
+
+    def column_copy(d, count):
+        size = count * chunks
+        return remote(colst.at[0, pl.ds(0, size)], colst.at[d, pl.ds(0, size)], CS_1 + d - 1, at_yc(d))
+
+    def column_counts(c):
+        return ((3, 5), (1, 5), (2, 3)) if c == 0 else ((2, 5), (3, 3), (1, 3))
+
+    statistics(2, send_rows)
+
+    joined = join(early, of_slot(2))
+    for q, v in enumerate((joined[0], joined[1], joined[4], joined[2], joined[3])):
+        colst[0, q * chunks : (q + 1) * chunks, :] = v
+
+    @pl.when(core == 0)
+    def _():
+        for d, count in column_counts(0):
+            column_copy(d, count).start()
+
+    @pl.when(core == 1)
+    def _():
+        for d, count in column_counts(1):
+            column_copy(d, count).start()
+
+    @pl.when((z == 0) & (core == 1))
     def _():
         @pl.when(high == 1)
         def _():
@@ -329,77 +379,92 @@
         pl.semaphore_wait(hello, depth - 1)
         loop(1, depth, lambda to: greet(go, at_z(to)))
 
-    def combine(ref, at, count, w):
-        ms, ls, es, hits = (
-            [ref[d, (q * count + at[d]) * per : (q * count + at[d] + 1) * per, :] for d in range(count)]
-            for q in range(4)
-        )
+    def tiles(ref, count, q):
+        size = count * per
+        return [ref[d, q * size : (q + 1) * size, :] for d in range(count)]
+
+    def combine(ref, count):
+        ms, ls = tiles(ref, count, 0), tiles(ref, count, 1)
         m = functools.reduce(jnp.maximum, ms)
         scales = [jnp.exp2(mi - m) for mi in ms]
-        l = sum(li * si for li, si in zip(ls, scales))
+        return m, sum(li * si for li, si in zip(ls, scales)), scales
+
+    def share(ref, count, w, es, hits, stats):
+        m, l, scales = stats
+        ms, ls = tiles(ref, count, 0), tiles(ref, count, 1)
         e = sum(si * (ei + (mi - m) * li) for mi, li, ei, si in zip(ms, ls, es, scales))
-        return m, l, w * (e / l - (sum(hits) - m))
-
-    for c in cs_copies:
-        c.wait_recv()
-    columns = []
-    for b in range(nyc):
-        at = [b ^ d for d in range(nyc)]
-        w = sum(colst[d, (4 * nyc + at[d]) * per : (4 * nyc + at[d] + 1) * per, :] for d in range(nyc))
-        columns.append(combine(colst, at, nyc, w) + (w,))
-    w_rows = [
-        jnp.concatenate([wp[r, 0:1, h * 128 : (h + 1) * 128] for h in range(per)], axis=0) for r in range(nx)
-    ]
-    for c in rs_copies:
-        c.wait_recv()
-    rows_ = [combine(rowst, [(r - d) % nx for d in range(nx)], nx, w_rows[r]) + (w_rows[r],) for r in range(nx)]
+        return w * (e / l - (sum(hits) - m))
+
+    @pl.when(core == 0)
+    def _():
+        for d in (1, 2, 3):
+            column_copy(d, 3).wait_recv()
+            row_copy(d, 2).wait_recv()
+
+    @pl.when(core == 1)
+    def _():
+        for d in (1, 2, 3):
+            column_copy(d, 5).wait_recv()
+            row_copy(d, 4).wait_recv()
 
     def line(v):
         v = jnp.sum(jnp.sum(v, axis=0, keepdims=True), axis=1, keepdims=True)
         return jnp.broadcast_to(v, (1, 128))
 
-    first_half = lane < 64
-    row_line = jnp.where(first_half, line(sum(v[2] for v in rows_)) * math.log(2.0), line(sum(w_rows)))
-    column_line = jnp.where(first_half, line(sum(v[2] for v in columns)) * math.log(2.0), 0.0)
-    mine[0] = row_line + column_line
-    mine[1] = row_line
-    mine[2] = column_line
-
-    relations = 14
+    relations = 10
 
     def part_copy(r):
         return pltpu.make_async_remote_copy(
-            src_ref=mine.at[0 if r < 2 else 1 if r < 8 else 2], dst_ref=parts_in.at[z * relations + r],
+            src_ref=mine.at[0 if r < 2 else 1 if r < 4 else 2], dst_ref=parts_in.at[z * relations + r],
             send_sem=part_send.at[r], recv_sem=part_recv.at[0], device_id=at_plane(r), device_id_type=MESH,
         )
 
-    own_part = pltpu.make_async_copy(mine.at[0], parts_in.at[0], part_recv.at[0])
-    others = (11, 12, 13, 8, 9, 10, 5, 6, 7, 1, 2, 3, 4)
-
-    @pl.when(z > 0)
-    def _():
-        pl.semaphore_wait(go, 1)
-        part_copy(12).start()
-        part_copy(0).start()
-
-    @pl.when(z == 0)
-    def _():
-        own_part.start()
-        part_copy(12).start()
-
-    for r in others:
-        if r != 12:
+    others = (8, 7, 9, 5, 4, 6, 3, 1, 2)
+
+    @pl.when(core == 1)
+    def _():
+        weights_copy.wait_recv()
+        for d in range(nx):
+            to_core_1(d).wait_recv()
+        row_share = share(rowst, nx, w_rows[...], tiles(rowst, nx, 2), tiles(rowst, nx, 3), combine(rowst, nx))
+        other_share = share(
+            other_rowst, nx, other_w[...], tiles(other_rowst, nx, 2), tiles(other_rowst, nx, 3),
+            combine(other_rowst, nx),
+        )
+        column_share = share(
+            colst, nyc, sum(tiles(colst, nyc, 2)), tiles(colst, nyc, 3), tiles(colst, nyc, 4),
+            combine(colst, nyc),
+        )
+        first_half = lane < 64
+        row_line = jnp.where(
+            first_half, line(row_share + other_share) * math.log(2.0), line(w_rows[...] + other_w[...])
+        )
+        column_line = jnp.where(first_half, line(column_share) * math.log(2.0), 0.0)
+        mine[0] = row_line + column_line
+        mine[1] = row_line
+        mine[2] = column_line
+
+        @pl.when(z > 0)
+        def _():
+            pl.semaphore_wait(go, 1)
+            part_copy(0).start()
+
+        @pl.when(z == 0)
+        def _():
+            pltpu.make_async_copy(mine.at[0], parts_in.at[0], part_recv.at[0]).start()
+
+        for r in others:
             part_copy(r).start()
 
-    b_rows = []
-    for m, l, _, w in columns:
-        v = m + jnp.log2(l / w)
-        b_rows += [v[h : h + 1, :] for h in range(per)]
+    m, l, _ = combine(colst, nyc)
+    b_tile[...] = m + jnp.log2(l / sum(tiles(colst, nyc, 2)))
+    m, l, _ = combine(rowst, nx)
+    a_rows[...] = m + jnp.log2(l / w_rows[...])
+    b_rows = [b_tile[pl.ds(column_place(c), 1), :] for c in range(chunks)]
     for r in (2, 1, 3, 0):
-        m, l, _, w = rows_[r]
-        a = m + jnp.log2(l / w)
         for h in range(per):
-            acol[r * n + h * 128 : r * n + (h + 1) * 128, :] = jnp.broadcast_to(a[h : h + 1, :], (128, 128)).T
+            a = a_rows[pl.ds(row_place(r, h), 1), :]
+            acol[r * n + h * 128 : r * n + (h + 1) * 128, :] = jnp.broadcast_to(a, (128, 128)).T
 
     def gradients(slot):
         def step(i, carry):
@@ -462,6 +527,12 @@
     own_gi[...] = item_part(0)
     gi_c0.wait_recv()
     own_gi[...] = own_gi[...] + got_core_0[...].astype(F32)
+    def all_copy(to, c):
+        return pltpu.make_async_remote_copy(
+            src_ref=totals, dst_ref=totals, send_sem=all_send.at[2 * to + c], recv_sem=all_recv.at[0],
+            device_id=at_z(to, c), device_id_type=MESH,
+        )
+
     gu_l0.wait_recv()
     gu_r1.wait_recv()
     gu_r0.wait_recv()
@@ -472,31 +543,52 @@
 
     for c in started:
         c.wait_send()
-    for r in others:
-        part_copy(r).wait_send()
-
-    @pl.when(z > 0)
-    def _():
-        part_copy(0).wait_send()
-
-    def all_copy(to):
-        return pltpu.make_async_remote_copy(
-            src_ref=totals, dst_ref=totals, send_sem=all_send.at[to], recv_sem=all_recv.at[0],
-            device_id=at_z(to), device_id_type=MESH,
-        )
-
-    @pl.when(z == 0)
+    @pl.when(core == 0)
+    def _():
+        weights_copy.wait_send()
+        for d in range(nx):
+            to_core_1(d).wait_send()
+        for d in (1, 2, 3):
+            row_copy(d, 2).wait_send()
+        for d, count in column_counts(0):
+            column_copy(d, count).wait_send()
+
+    @pl.when(core == 1)
+    def _():
+        for d in (1, 2, 3):
+            row_copy(d, 4).wait_send()
+        for d, count in column_counts(1):
+            column_copy(d, count).wait_send()
+        for r in others:
+            part_copy(r).wait_send()
+
+        @pl.when(z > 0)
+        def _():
+            part_copy(0).wait_send()
+
+    @pl.when((z == 0) & (core == 1))
     def _():
         pltpu.make_async_copy(parts_in, parts_in, part_recv.at[0]).wait()
         sums = [parts_in[i] for i in range(relations * depth)]
         while len(sums) > 1:
             sums = [sum(sums[i : i + 2]) for i in range(0, len(sums), 2)]
         totals[...] = sums[0]
-        loop(1, depth, lambda to: all_copy(to).start())
-
-    @pl.when(z > 0)
-    def _():
-        all_copy(0).wait_recv()
+
+        for to in range(1, min(5, depth)):
+            all_copy(to, 0).start()
+            all_copy(to, 1).start()
+        all_copy(0, 0).start()
+        loop(5, depth, lambda to: all_copy(to, 1).start())
+
+    @pl.when((z > 0) | (core == 0))
+    def _():
+        all_copy(0, 0).wait_recv()
+
+    pass_on_totals = (z > 4) & (core == 1)
+
+    @pl.when(pass_on_totals)
+    def _():
+        all_copy(z, 0).start()
 
     sums = totals[...]
     weight = jnp.broadcast_to(sums[:, 64:65], (1, 128))
@@ -505,9 +597,15 @@
     factor = (rows_total / weight) * (k[:, 0:128] * math.log(2.0))
     factor_out[...] = jnp.concatenate([factor] * (width // 128), axis=1)
 
-    @pl.when(z == 0)
-    def _():
-        loop(1, depth, lambda to: all_copy(to).wait_send())
+    @pl.when((z == 0) & (core == 1))
+    def _():
+        all_copy(0, 0).wait_send()
+        loop(1, min(5, depth), lambda to: all_copy(to, 0).wait_send())
+        loop(1, depth, lambda to: all_copy(to, 1).wait_send())
+
+    @pl.when(pass_on_totals)
+    def _():
+        all_copy(z, 0).wait_send()
 
 
 def body(users, items, weights, positives, log_scale):
@@ -545,7 +643,14 @@
             V((n, 128), F32),
             V((3, n, 128), F32),
             V((nx, 4 * nx * n // 128, 128), F32),
-            V((nyc, 5 * nyc * n // 128, 128), F32),
+            V((nx, 4 * nx * n // 128, 128), F32),
+            V((rows // 128, 128), F32),
+            V((nyc, 5 * cols // 128, 128), F32),
+            V((nx, 5 * cols // 128, 128), F32),
+            V((4, 8 * cols // 128, 128), F32),
+            V((rows // 128, 128), F32),
+            V((rows // 128, 128), F32),
+            V((cols // 128, 128), F32),
             pltpu.SMEM((1,), F32),
             V((n, width), BF16),
             V((half, width), BF16),
@@ -564,14 +669,14 @@
             V((n, width), BF16),
             V((n, width), BF16),
             V((3, 1, 128), F32),
-            V((14 * n_dp // 2, 1, 128), F32),
+            V((10 * n_dp // 2, 1, 128), F32),
             V((1, 128), F32),
             pltpu.SemaphoreType.DMA((5,)),
             pltpu.SemaphoreType.DMA((TRANSFERS,)),
             pltpu.SemaphoreType.DMA((TRANSFERS,)),
-            pltpu.SemaphoreType.DMA((14,)),
+            pltpu.SemaphoreType.DMA((10,)),
             pltpu.SemaphoreType.DMA((1,)),
-            pltpu.SemaphoreType.DMA((n_dp // 2,)),
+            pltpu.SemaphoreType.DMA((n_dp,)),
             pltpu.SemaphoreType.DMA((1,)),
             pltpu.SemaphoreType.REGULAR,
             pltpu.SemaphoreType.REGULAR,

time: 45.5 us -> 44.9 us (0.987)
  the two profiles are of different devices: /device:TPU:32 before, /device:TPU:1 now
where the time goes in v6:
time: 44.9 us; the launch traced here: 44.7 us
  Pallas kernels  42 us (94%)
  between operations  1.29 us (3%)
  other arithmetic  0.91 us (2%)
  local copies, waits for them, and re-layouts  0.51 us (1%)
    pallas_call x1, Pallas kernels, body(): pl.pallas_call(functools.partial(kernel, nx, nyc, n_dp, n_blk), out_shape...  42 us
    broadcast_in_dim x1, other arithmetic, body(): (gi * factor).astype(BF16)[None]  0.91 us

profile of v6, /device:TPU:1, one launch (start us, length us, event | category | flops | bytes accessed | tf_op | source)
XLA Modules:
  0.0 44.7 jit_solution(7806953615230552639)
XLA Ops:
  1.3 42.0 %loss_gradients.1 = (f32[256,512]{1,0:T(8,128)S(1)}, f32[256,512]{1,0:T(8,128)S(1)}, f32[8,128]{1,0:T(8,128)S(1)}, f32[1,512]{1,0:T(1,128)S(1)}) custom-call(bf16[256,512]{1,0:T(8,128)(2,1)} %bitcast.9, bf16[256,512]{1,0:T(8,128)(2,1)} %bitcast.10, f32[1,256]{1,0:T(1,128)} %weights.1, s32[1,256]{1,0:T(1,128)} %positives.1, f32[1]{0:T(128)S(6)} %copy.8.log_scale), custom_call_target="tpu_custom_call" | custom-call | flops 3221225472 | bytes 1048576 | tf_op jit(solution)/shard_map/loss_gradients/pallas_call | solution.py:622
  43.3 0.5 %slice.3 = f32[1,1]{1,0:T(1,128)} slice(f32[8,128]{1,0:T(8,128)S(1)} %get-tuple-element.10), slice={[0:1], [0:1]} | slice | bytes 8 | tf_op jit(solution)/shard_map/slice | solution.py:694
  43.8 0.9 %fusion.1 = (bf16[1,256,512]{2,1,0:T(8,128)(2,1)}, bf16[1,256,512]{2,1,0:T(8,128)(2,1)}) fusion(f32[256,512]{1,0:T(8,128)S(1)} %get-tuple-element.9, f32[512]{0:T(512)S(1)} %bitcast.8, f32[256,512]{1,0:T(8,128)S(1)} %get-tuple-element.7), kind=kLoop, calls=%fused_computation.3 | loop fusion | flops 524288 | bytes 1574912 | tf_op jit(solution)/shard_map/broadcast_in_dim | solution.py:694

commit v7 on v6

--- a/solution.py
+++ b/solution.py
@@ -12,7 +12,7 @@
 F32 = jnp.float32
 BF16 = jnp.bfloat16
 LOW = -3.0e38
-CHUNK = 32
+CHUNK = 64
 
 (
     U_RIGHT_0, U_LEFT_1, U_RIGHT_1, U_LEFT_0, U_RELAY_RIGHT, U_RELAY_LEFT,

time: 44.9 us -> 44.9 us (level)
  no operation moved by 1% of the time
where the time goes in v7:
time: 44.9 us; the launch traced here: 44.7 us
  Pallas kernels  42 us (94%)
  between operations  1.29 us (3%)
  other arithmetic  0.91 us (2%)
  local copies, waits for them, and re-layouts  0.51 us (1%)
    pallas_call x1, Pallas kernels, body(): pl.pallas_call(functools.partial(kernel, nx, nyc, n_dp, n_blk), out_shape...  42 us
    broadcast_in_dim x1, other arithmetic, body(): (gi * factor).astype(BF16)[None]  0.91 us

profile of v7, /device:TPU:1, one launch (start us, length us, event | category | flops | bytes accessed | tf_op | source)
XLA Modules:
  0.0 44.7 jit_solution(8681222534157410833)
XLA Ops:
  1.3 42.0 %loss_gradients.1 = (f32[256,512]{1,0:T(8,128)S(1)}, f32[256,512]{1,0:T(8,128)S(1)}, f32[8,128]{1,0:T(8,128)S(1)}, f32[1,512]{1,0:T(1,128)S(1)}) custom-call(bf16[256,512]{1,0:T(8,128)(2,1)} %bitcast.9, bf16[256,512]{1,0:T(8,128)(2,1)} %bitcast.10, f32[1,256]{1,0:T(1,128)} %weights.1, s32[1,256]{1,0:T(1,128)} %positives.1, f32[1]{0:T(128)S(6)} %copy.8.log_scale), custom_call_target="tpu_custom_call" | custom-call | flops 3221225472 | bytes 1048576 | tf_op jit(solution)/shard_map/loss_gradients/pallas_call | solution.py:622
  43.3 0.5 %slice.3 = f32[1,1]{1,0:T(1,128)} slice(f32[8,128]{1,0:T(8,128)S(1)} %get-tuple-element.10), slice={[0:1], [0:1]} | slice | bytes 8 | tf_op jit(solution)/shard_map/slice | solution.py:694
  43.8 0.9 %fusion.1 = (bf16[1,256,512]{2,1,0:T(8,128)(2,1)}, bf16[1,256,512]{2,1,0:T(8,128)(2,1)}) fusion(f32[256,512]{1,0:T(8,128)S(1)} %get-tuple-element.9, f32[512]{0:T(512)S(1)} %bitcast.8, f32[256,512]{1,0:T(8,128)S(1)} %get-tuple-element.7), kind=kLoop, calls=%fused_computation.3 | loop fusion | flops 524288 | bytes 1574912 | tf_op jit(solution)/shard_map/broadcast_in_dim | solution.py:694
